TPU v7x, 256 devices: a whole 4x4x8 slice. The times are simulated.
256 devices in a mesh: dp: 4 (over x_hi, core), prompt: 16 (over z, x_lo), resp: 4 (over y).
Axes of the slice: x: 4 (x_hi: 2, x_lo: 2; x = x_hi * 2 + x_lo), y: 4, z: 8, core: 2. Of those that a mesh axis runs over, the one named last changes fastest.
Arguments:
- prompt_q: bfloat16 [4096, 4096], P(('prompt', 'resp'), 'dp'), may hold values from -6 to 6
- prompt_key_value: bfloat16 [2, 4096, 512], P(None, ('prompt', 'resp'), 'dp'), may hold values from -6 to 6
- resp_q: bfloat16 [2, 2048, 4096], P(None, ('prompt', 'resp'), 'dp'), may hold values from -6 to 6
- response_key_value: bfloat16 [2, 2, 2048, 512], P(None, None, ('prompt', 'resp'), 'dp'), may hold values from -6 to 6
- labels: int32 [2, 2048], P(None, ('prompt', 'resp')), may hold values 0 or 1
- logp_rest: float32 [2, 2048], P(None, ('prompt', 'resp')), may hold values from -0.75 to 0.75
- resp_probe: bfloat16 [2, 2048, 4096], P(None, ('prompt', 'resp'), 'dp'), may hold values from -0.75 to 0.75
- prompt_probe: bfloat16 [4096, 4096], P(('prompt', 'resp'), 'dp'), may hold values from -6 to 6
Outputs:
- prompt_out: bfloat16 [4096, 4096], P(('prompt', 'resp'), 'dp')
- resp_out: bfloat16 [2, 2048, 4096], P(None, ('prompt', 'resp'), 'dp')
- prompt_dq: bfloat16 [4096, 4096], P(('prompt', 'resp'), 'dp')
- resp_dq: bfloat16 [2, 2048, 4096], P(None, ('prompt', 'resp'), 'dp')
- prompt_dkv: bfloat16 [2, 4096, 512], P(None, ('prompt', 'resp'), 'dp')
- resp_dkv: bfloat16 [2, 2, 2048, 512], P(None, None, ('prompt', 'resp'), 'dp')
- dpo_loss: float32 [], replicated
All inputs are finite; a program needn't handle non-finite values. No bound on the sum of `labels` on one device may be relied on, other than what follows from the above.
Results may differ from a plain program's by a relative error of at most 0.039.
Values may be sent and summed in bfloat16 or wider, within the bound.
No kernel may reach another device: no remote copies, remote signals or barrier semaphores. Data moves between devices by JAX's collectives and lax.ppermute only.
A program may use at most 128 MiB of HBM per device.

v0:
```python
import math

import jax
import jax.numpy as jnp
from jax import lax
from jax.sharding import PartitionSpec as P

QUERY_HEADS = 32
KEY_VALUE_HEADS = 4
HEAD_SIZE = 128


NEG_FILL = -1e30
BETA = 0.1


def visible_scores(queries, key_rows, query_pos, key_start, key_block, softmax_scale):
    kblock = lax.dynamic_slice_in_dim(key_rows, key_start, key_block, 0)
    raw_scores = (
        jnp.einsum("qkgd,nkd->kgqn", queries, kblock, preferred_element_type=jnp.float32)
        * softmax_scale
    )
    key_pos = key_start + jnp.arange(key_block, dtype=jnp.int32)
    return jnp.where(query_pos[:, None] >= key_pos[None, :], raw_scores, NEG_FILL)


def attend_forward(queries, key_rows, value_rows, first_pos, block_trips, key_block):
    query_rows, kv_heads, query_groups, head_width = queries.shape
    softmax_scale = head_width ** (-0.5)
    query_pos = first_pos + jnp.arange(query_rows, dtype=jnp.int32)

    def stats_step(block_step, state_pair):
        peak_score, row_total = state_pair
        masked = visible_scores(
            queries, key_rows, query_pos, block_step * key_block, key_block, softmax_scale
        )
        new_peak = jnp.maximum(peak_score, jnp.max(masked, axis=-1))
        row_total = row_total * jnp.exp(peak_score - new_peak) + jnp.sum(
            jnp.exp(masked - new_peak[..., None]), axis=-1
        )
        return (new_peak, row_total)

    start_peak = jnp.full((kv_heads, query_groups, query_rows), NEG_FILL, jnp.float32)
    peak_score, row_total = lax.fori_loop(
        0, block_trips, stats_step, (start_peak, jnp.zeros_like(start_peak))
    )
    log_total = peak_score + jnp.log(row_total)

    def out_step(block_step, out_acc):
        key_start = block_step * key_block
        masked = visible_scores(queries, key_rows, query_pos, key_start, key_block, softmax_scale)
        vblock = lax.dynamic_slice_in_dim(value_rows, key_start, key_block, 0)
        weights = jnp.exp(masked - log_total[..., None]).astype(jnp.bfloat16)
        return out_acc + jnp.einsum(
            "kgqn,nkd->qkgd", weights, vblock, preferred_element_type=jnp.float32
        )

    out_acc = lax.fori_loop(0, block_trips, out_step, jnp.zeros(queries.shape, jnp.float32))
    return (out_acc.astype(jnp.bfloat16), log_total)


def attend_backward(
    queries,
    key_rows,
    value_rows,
    outputs,
    grad_out,
    log_total,
    first_pos,
    block_trips,
    key_block,
    grad_terms,
):
    query_rows, kv_heads, query_groups, head_width = queries.shape
    softmax_scale = head_width ** (-0.5)
    query_pos = first_pos + jnp.arange(query_rows, dtype=jnp.int32)
    row_delta = jnp.sum(
        grad_out.astype(jnp.float32) * outputs.astype(jnp.float32), axis=-1
    ).transpose(1, 2, 0)

    def grad_step(block_step, state_pair):
        dquery, grad_terms = state_pair
        key_start = block_step * key_block
        masked = visible_scores(queries, key_rows, query_pos, key_start, key_block, softmax_scale)
        kblock = lax.dynamic_slice_in_dim(key_rows, key_start, key_block, 0)
        vblock = lax.dynamic_slice_in_dim(value_rows, key_start, key_block, 0)
        prob_full = jnp.exp(masked - log_total[..., None])
        weights = prob_full.astype(jnp.bfloat16)
        dprob_block = jnp.einsum(
            "qkgd,nkd->kgqn", grad_out, vblock, preferred_element_type=jnp.float32
        )
        dscore = (prob_full * (dprob_block - row_delta[..., None])).astype(jnp.bfloat16)
        dquery = dquery + jnp.einsum(
            "kgqn,nkd->qkgd", dscore, kblock, preferred_element_type=jnp.float32
        )
        dkey_block = (
            jnp.einsum("kgqn,qkgd->nkd", dscore, queries, preferred_element_type=jnp.float32)
            * softmax_scale
        )
        dvalue = jnp.einsum("kgqn,qkgd->nkd", weights, grad_out, preferred_element_type=jnp.float32)
        old_terms = lax.dynamic_slice_in_dim(grad_terms, key_start, key_block, 1)
        grad_terms = lax.dynamic_update_slice_in_dim(
            grad_terms, old_terms + jnp.stack([dkey_block, dvalue]), key_start, 1
        )
        return (dquery, grad_terms)

    dquery, grad_terms = lax.fori_loop(
        0, block_trips, grad_step, (jnp.zeros(queries.shape, jnp.float32), grad_terms)
    )
    return ((dquery * softmax_scale).astype(jnp.bfloat16), grad_terms)


def per_device(
    prompt_q,
    prompt_key_value,
    resp_q,
    response_key_value,
    labels,
    logp_rest,
    resp_probe,
    prompt_probe,
):
    prompt_rows = prompt_q.shape[0]
    resp_rows = resp_q.shape[1]
    kv_heads = prompt_key_value.shape[2] // HEAD_SIZE
    query_groups = QUERY_HEADS // KEY_VALUE_HEADS
    prompt_pool, resp_pool = (
        lax.all_gather(prompt_key_value, ("prompt", "resp"), axis=1, tiled=True),
        lax.all_gather(response_key_value, ("prompt", "resp"), axis=2, tiled=True),
    )
    shard_count = lax.axis_size("prompt") * lax.axis_size("resp")
    shard_index = lax.axis_index("prompt") * lax.axis_size("resp") + lax.axis_index("resp")
    block_unit = math.gcd(prompt_rows, resp_rows)
    factor = 1
    for level in range(12):
        if factor * 2 <= shard_count and block_unit * factor * 2 <= 512:
            factor = factor * 2
    key_block = block_unit * factor
    prompt_grand_sum = prompt_pool.shape[1]
    response_grand_sum = resp_pool.shape[2]
    prompt_keys = prompt_pool[0].reshape(prompt_grand_sum, kv_heads, HEAD_SIZE)
    prompt_values = prompt_pool[1].reshape(prompt_grand_sum, kv_heads, HEAD_SIZE)
    resp_keys = resp_pool[0].reshape(2, response_grand_sum, kv_heads, HEAD_SIZE)
    resp_values = resp_pool[1].reshape(2, response_grand_sum, kv_heads, HEAD_SIZE)
    resp_query = resp_q.reshape(2, resp_rows, kv_heads, query_groups, HEAD_SIZE)
    resp_first = prompt_grand_sum + shard_index * resp_rows
    resp_trips = (resp_first + resp_rows - 1) // key_block + 1
    joined_keys = [
        jnp.concatenate([prompt_keys, resp_keys[side_index]], axis=0) for side_index in range(2)
    ]
    joined_values = [
        jnp.concatenate([prompt_values, resp_values[side_index]], axis=0) for side_index in range(2)
    ]
    side_outs = []
    side_stats = []
    for side_index in range(2):
        side_out, side_lse = attend_forward(
            resp_query[side_index],
            joined_keys[side_index],
            joined_values[side_index],
            resp_first,
            resp_trips,
            key_block,
        )
        side_outs.append(side_out)
        side_stats.append(side_lse)
    resp_out = jnp.stack(side_outs).reshape(2, resp_rows, -1)
    sign_row = jnp.array([1.0, -1.0], dtype=jnp.float32)
    counted = labels.astype(jnp.float32) * sign_row[:, None]
    probe_score = jnp.sum(resp_out.astype(jnp.float32) * resp_probe.astype(jnp.float32), axis=-1)
    partial_margin = jnp.sum(counted * (logp_rest / lax.axis_size("dp") + probe_score))
    margin = BETA * lax.psum(partial_margin, ("dp", "prompt", "resp"))
    dpo_loss = jax.nn.softplus(-margin)
    weight = -BETA * jax.nn.sigmoid(-margin)
    resp_grad = ((weight * counted)[..., None] * resp_probe.astype(jnp.float32)).astype(
        jnp.bfloat16
    )
    prompt_grad = (weight * prompt_probe.astype(jnp.float32)).astype(jnp.bfloat16)
    resp_dgrad = resp_grad.reshape(2, resp_rows, kv_heads, query_groups, HEAD_SIZE)
    side_dq = []
    side_terms = []
    for side_index in range(2):
        empty_terms = jnp.zeros(
            (2, prompt_grand_sum + response_grand_sum, kv_heads, HEAD_SIZE), jnp.float32
        )
        dq_side, terms_side = attend_backward(
            resp_query[side_index],
            joined_keys[side_index],
            joined_values[side_index],
            side_outs[side_index],
            resp_dgrad[side_index],
            side_stats[side_index],
            resp_first,
            resp_trips,
            key_block,
            empty_terms,
        )
        side_dq.append(dq_side)
        side_terms.append(terms_side)
    resp_dq = jnp.stack(side_dq).reshape(2, resp_rows, -1)
    prompt_terms = side_terms[0][:, :prompt_grand_sum] + side_terms[1][:, :prompt_grand_sum]
    resp_terms = jnp.stack(
        [side_terms[0][:, prompt_grand_sum:], side_terms[1][:, prompt_grand_sum:]], axis=1
    )
    prompt_query = prompt_q.reshape(prompt_rows, kv_heads, query_groups, HEAD_SIZE)
    prompt_dgrad = prompt_grad.reshape(prompt_rows, kv_heads, query_groups, HEAD_SIZE)
    own_first = shard_index * prompt_rows
    own_trips = (own_first + prompt_rows - 1) // key_block + 1
    own_out, own_lse = attend_forward(
        prompt_query, prompt_keys, prompt_values, own_first, own_trips, key_block
    )
    own_dq, prompt_terms = attend_backward(
        prompt_query,
        prompt_keys,
        prompt_values,
        own_out,
        prompt_dgrad,
        own_lse,
        own_first,
        own_trips,
        key_block,
        prompt_terms,
    )
    prompt_out = own_out.reshape(prompt_rows, -1)
    prompt_dq = own_dq.reshape(prompt_rows, -1)
    flat_prompt = prompt_terms.reshape(2, prompt_grand_sum, -1)
    flat_resp = resp_terms.reshape(2, 2, response_grand_sum, -1)
    prompt_sum, resp_sum = (
        lax.psum_scatter(flat_prompt, ("prompt", "resp"), scatter_dimension=1, tiled=True),
        lax.psum_scatter(flat_resp, ("prompt", "resp"), scatter_dimension=2, tiled=True),
    )
    return (
        prompt_out,
        resp_out,
        prompt_dq,
        resp_dq,
        prompt_sum.astype(jnp.bfloat16),
        resp_sum.astype(jnp.bfloat16),
        dpo_loss,
    )


def solution(mesh):
    placed = (
        P(("prompt", "resp"), "dp"),
        P(None, ("prompt", "resp"), "dp"),
        P(None, ("prompt", "resp"), "dp"),
        P(None, None, ("prompt", "resp"), "dp"),
        P(None, ("prompt", "resp")),
        P(None, ("prompt", "resp")),
        P(None, ("prompt", "resp"), "dp"),
        P(("prompt", "resp"), "dp"),
    )
    return jax.shard_map(
        per_device,
        mesh=mesh,
        in_specs=placed,
        out_specs=(
            P(("prompt", "resp"), "dp"),
            P(None, ("prompt", "resp"), "dp"),
            P(("prompt", "resp"), "dp"),
            P(None, ("prompt", "resp"), "dp"),
            P(None, ("prompt", "resp"), "dp"),
            P(None, None, ("prompt", "resp"), "dp"),
            P(),
        ),
        check_vma=False,
    )
```

profile of v0, /device:TPU:4, one launch (start us, length us, event | category | flops | bytes accessed | tf_op | source)
XLA Modules:
  0.0 1618.6 jit_solution(8910997735445191975)
XLA Ops:
  10.6 301.6 %all-gather.3.cloned.1.call-done = bf16[2,4096,128]{2,1,0:T(8,128)(2,1)} async-done(((bf16[2,64,128]{2,1,0:T(8,128)(2,1)}), bf16[2,4096,128]{2,1,0:T(8,128)(2,1)}) %all-gather.3.cloned.1.call-update) | async-done | bytes 2097168 | tf_op jit(solution)/shard_map/all_gather | solution.py:128
  313.9 297.5 %all-gather.5.cloned.1.call-done = bf16[2,2,2048,128]{3,2,1,0:T(8,128)(2,1)} async-done(((bf16[2,2,32,128]{3,2,1,0:T(8,128)(2,1)}), bf16[2,2,2048,128]{3,2,1,0:T(8,128)(2,1)}) %all-gather.5.cloned.1.call-update) | async-done | bytes 2097168 | tf_op jit(solution)/shard_map/all_gather | solution.py:129
  613.1 8.4 pad_maximum_fusion
  621.4 14.5 while.113
  635.9 13.4 while.114
  649.4 14.5 while.115
  664.0 13.4 while.116
  678.4 92.2 %psum.7 = f32[]{:T(128)} all-reduce(f32[]{:T(128)} %multiply_reduce_fusion.3), channel_id=1, replica_groups=mesh['dp'=4,'prompt'=16,'resp'=4] {'dp','prompt','resp'}, use_global_device_ids=true, to_apply=%region_20.21 | all-reduce | flops 1 | bytes 8 | tf_op jit(solution)/shard_map/psum | solution.py:172
  773.9 3.1 broadcast.174.clone
  776.9 54.7 %while.118 = (s32[]{:T(128)}, f32[32,1,8,128]{3,0,2,1:T(8,128)S(1)}, f32[2,6144,1,128]{3,1,2,0:T(8,128)}, s32[]{:T(128)}, bf16[6144,1,128]{2,0,1:T(8,128)(2,1)},...) while((s32[]{:T(128)}, f32[32,1,8,128]{3,0,2,1:T(8,128)S(1)}, ...), condition=%wide.region_26.27_spmd.clone, body=%wide.region_25.26_spmd.clone.sunk | while | flops 169067040 | bytes 5413339 | solution.py:107
  799.2 1.9 fusion.303
  805.3 2.0 fusion.303
  811.4 2.0 fusion.303
  817.5 2.0 fusion.303
  823.6 1.9 fusion.303
  829.7 2.0 fusion.303
  831.6 3.1 broadcast.174.clone.1
  834.7 54.6 %while.117 = (s32[]{:T(128)}, f32[32,1,8,128]{3,0,2,1:T(8,128)S(1)}, f32[2,6144,1,128]{3,1,2,0:T(8,128)}, s32[]{:T(128)}, bf16[6144,1,128]{2,0,1:T(8,128)(2,1)},...) while((s32[]{:T(128)}, f32[32,1,8,128]{3,0,2,1:T(8,128)S(1)}, ...), condition=%wide.region_23.24_spmd.clone, body=%wide.region_22.23_spmd.clone.sunk | while | flops 169067040 | bytes 5413339 | solution.py:107
  869.2 2.0 fusion.288
  889.4 5.9 slice_add_fusion
  895.2 4.0 while.119
  902.7 2.2 maximum_bitcast_fusion
  907.4 381.3 %reduce-scatter.3.cloned.1.call-done = f32[2,64,128]{2,1,0:T(8,128)} async-done(((f32[2,4096,128]{2,1,0:T(8,128)}), f32[2,64,128]{2,1,0:T(8,128)}) %reduce-scatter.3.cloned.1.call-update) | async-done | bytes 65552 | tf_op jit(solution)/shard_map/reduce_scatter | solution.py:229
  1290.1 319.3 %reduce-scatter.5.cloned.1.call-done = f32[2,2,32,128]{3,2,1,0:T(8,128)} async-done(((f32[2,2,2048,128]{3,2,1,0:T(8,128)}), f32[2,2,32,128]{3,2,1,0:T(8,128)}) %reduce-scatter.5.cloned.1.call-update) | async-done | bytes 65552 | tf_op jit(solution)/shard_map/reduce_scatter | solution.py:230
  (477 shorter events, 172.2 us)
Async XLA Ops:
  7.2 305.0 %all-gather.3.cloned.1.call-start = ((), (), s32[]{:S(2)}) async-start(), calls=%async_computation.2 | async-start | bytes 2129920 | tf_op jit(solution)/shard_map/all_gather | solution.py:128
  7.9 603.5 %all-gather.5.cloned.1.call-start = ((), (), s32[]{:S(2)}) async-start(), calls=%async_computation.3 | async-start | bytes 2129920 | tf_op jit(solution)/shard_map/all_gather | solution.py:129
  8.7 1280.0 %reduce-scatter.3.cloned.1.call-start = ((), (), s32[]{:S(2)}) async-start(), calls=%async_computation.4 | async-start | bytes 4259840 | tf_op jit(solution)/shard_map/reduce_scatter | solution.py:229
  664.0 13.6 copy-start
  664.0 13.7 copy-start.3
  664.0 13.7 copy-start.4
  664.0 13.7 copy-start.5
  677.4 94.4 %copy-start.2 = (bf16[64,1024]{1,0:T(8,128)(2,1)S(1)}, bf16[64,1024]{1,0:T(8,128)(2,1)}, u32[]{:S(2)}) copy-start(bf16[64,1024]{1,0:T(8,128)(2,1)} %param.34) | copy-start | bytes 393220
  677.5 94.4 %copy-start.1 = (bf16[2,32,1024]{2,1,0:T(8,128)(2,1)}, bf16[2,32,1024]{2,1,0:T(8,128)(2,1)S(1)}, u32[]{:S(2)}) copy-start(bf16[2,32,1024]{2,1,0:T(8,128)(2,1)S(1)} %constant_dynamic-update-slice_fusion) | copy-start | bytes 393220
  899.2 710.2 %reduce-scatter.5.cloned.1.call-start = ((), (), s32[]{:S(2)}) async-start(), calls=%async_computation.5 | async-start | bytes 4259840 | tf_op jit(solution)/shard_map/reduce_scatter | solution.py:230
Sparse Core Ops, SparseCore 0:
  9.8 302.3 all-gather.2
  314.0 297.3 all-gather.4
  899.3 389.2 reduce-scatter.2
  1291.2 318.2 reduce-scatter.4
where the time goes:
time: 1620 us
  waiting for transfers between devices  1300 us (80%)
  matrix products  120 us (7%)
  blocking collectives  92.2 us (6%)
  other arithmetic  68 us (4%)
  local copies, waits for them, and re-layouts  16.8 us (1%)
  between operations  16.2 us (1%)
    reduce_scatter x1, waiting for transfers between devices, per_device(): lax.psum_scatter(flat_prompt, ('prompt', 'resp'), scatter_dimension=1, ti...  381 us
    reduce_scatter x1, waiting for transfers between devices, per_device(): lax.psum_scatter(flat_resp, ('prompt', 'resp'), scatter_dimension=2, tile...  319 us
    all_gather x1, waiting for transfers between devices, per_device(): lax.all_gather(prompt_key_value, ('prompt', 'resp'), axis=1, tiled=True)  302 us
    all_gather x1, waiting for transfers between devices, per_device(): lax.all_gather(response_key_value, ('prompt', 'resp'), axis=2, tiled=True)  298 us
    psum x1, blocking collectives, per_device(): margin = BETA * lax.psum(partial_margin, ('dp', 'prompt', 'resp'))  92.2 us
    dot_general x38, matrix products, visible_scores(): jnp.einsum('qkgd,nkd->kgqn', queries, kblock, preferred_element_type=jnp....  43.5 us
    dynamic_update_slice x19, other arithmetic, grad_step(): lax.dynamic_update_slice_in_dim(grad_terms, old_terms + jnp.stack([dkey_b...  36.8 us
  transfers between devices with their start and end apart: 4, of which 4 were waited for; matrix products, arithmetic and copies ran while one was open for 1% of the time, Pallas kernels for 0%

commit v1 on v0

v1 whole, which is shorter than its diff:
```python
import functools
import math

import jax
import jax.numpy as jnp
from jax import lax
from jax.experimental import pallas as pl
from jax.experimental.pallas import tpu as pltpu
from jax.sharding import PartitionSpec as P

QUERY_HEADS = 32
KEY_VALUE_HEADS = 4
HEAD_SIZE = 128
BETA = 0.1
HIDDEN = -1e30
FLOOR = -1e29
SCALE = HEAD_SIZE ** -0.5
SCALE2 = SCALE * math.log2(math.e)

HEADS = QUERY_HEADS // KEY_VALUE_HEADS
D = HEAD_SIZE
BF16 = jnp.bfloat16
F32 = jnp.float32
CHUNK = 256

NT = (((1,), (1,)), ((), ()))
TN = (((0,), (0,)), ((), ()))
NN = (((1,), (0,)), ((), ()))


def mm(a, b, dims):
    return lax.dot_general(a, b, dims, preferred_element_type=F32)


def counted_rows(labels):
    row = lax.broadcasted_iota(jnp.int32, labels.shape, 0)
    return labels.astype(F32) * jnp.where(row == 0, 1.0, -1.0)


def as_column(row):
    n = row.shape[1]
    r = lax.broadcasted_iota(jnp.int32, (n, n), 0)
    c = lax.broadcasted_iota(jnp.int32, (n, n), 1)
    return jnp.sum(jnp.where(r == c, jnp.broadcast_to(row, (n, n)), 0.0), axis=1, keepdims=True)


def pack_kernel(sizes, pq, pkv, rq, rkv, labels, probe, pprobe, qg, kvb):
    tp, tr, groups = sizes
    qg[0:tp] = pq[...]
    qg[tp + 2 * tr : 2 * tp + 2 * tr] = pprobe[...]
    counted = counted_rows(labels[...])
    for s in range(2):
        qg[tp + s * tr : tp + (s + 1) * tr] = rq[s]
        col = as_column(counted[s : s + 1])
        base = 2 * tp + 2 * tr + s * tr
        qg[base : base + tr] = (probe[s].astype(F32) * col).astype(BF16)
    for g in range(groups):
        for i in range(2):
            kvb[g, i * tp : (i + 1) * tp] = pkv[i]
            for s in range(2):
                base = 2 * tp + (2 * i + s) * tr
                kvb[g, base : base + tr] = rkv[i, s]


def tile_lanes(sizes, ways):
    tp, tr, _ = sizes
    half = ways // 2
    return [(0, 0, ways), (1, 0, ways), (-1, 0, half), (-1, half, ways)]


def limits(kind, first, last, rows, g, y):
    lanes = (last - first) * HEADS * rows
    lane = lax.broadcasted_iota(jnp.int32, (1, lanes), 1)
    src = first + lane // (HEADS * rows)
    t = lane % rows
    return g * rows + jnp.where(src == 0, t + 1, jnp.where(src > y, rows, 0))


def hide(s, start, lim):
    key = lax.broadcasted_iota(jnp.int32, s.shape, 0) + start
    return jnp.where(key < lim, s, HIDDEN)


def key_chunk(kv, chunk, rows, base):
    n = CHUNK // rows
    return kv[pl.ds(chunk * n, n), base : base + rows, :].reshape(CHUNK, D)


def offsets(kind, sizes):
    tp, tr, _ = sizes
    if kind < 0:
        return 0, tp
    return 2 * tp + kind * tr, 2 * tp + 2 * tr + kind * tr


def row_base(kind, sizes, ways):
    tp, tr, _ = sizes
    return 0 if kind < 0 else ways * HEADS * (tp + kind * tr)


def stats_lane(kind, sizes):
    tp, tr, _ = sizes
    return 0 if kind < 0 else HEADS * (tp + kind * tr)


def forward_kernel(sizes, ways, where, labels, logp, kv, *refs):
    qg = refs[:ways]
    qs, gs, ot, stats, s_scr = refs[ways:]
    tp, tr, groups = sizes
    g, y = where[0], where[1]
    counted = counted_rows(labels[...])
    rest = jnp.sum(counted * logp[...], axis=(0, 1), keepdims=True)

    for tile, (kind, first, last) in enumerate(tile_lanes(sizes, ways)):
        rows = tp if kind < 0 else tr
        qrow = 0 if kind < 0 else tp + kind * tr
        grow = qrow + tp + 2 * tr
        per = HEADS * rows
        lanes = (last - first) * per
        base = row_base(kind, sizes, ways) + first * per
        for j in range(first, last):
            for h in range(HEADS):
                at = base + (j - first) * per + h * rows
                qs[at : at + rows] = qg[j][qrow : qrow + rows, h * D : (h + 1) * D]
                gs[at : at + rows] = qg[j][grow : grow + rows, h * D : (h + 1) * D]
        q = qs[base : base + lanes]
        grad = gs[base : base + lanes]
        lim = limits(kind, first, last, rows, g, y)
        koff, voff = offsets(kind, sizes)
        n_prompt = groups * tp // CHUNK if kind >= 0 else 0
        per_chunk = CHUNK // rows
        n_own = g // per_chunk + 1

        def score_step(chunk, peak, rows_k, off, start, lim, masked):
            s = mm(key_chunk(kv, chunk, rows_k, off), q, NT) * SCALE2
            if masked:
                s = hide(s, chunk * CHUNK, lim)
            s_scr[pl.ds(start + chunk * CHUNK, CHUNK), :] = s
            return jnp.maximum(peak, jnp.max(s.reshape(CHUNK // 8, 8, lanes), axis=0))

        peak = jnp.full((8, lanes), FLOOR, F32)
        if n_prompt:
            peak = lax.fori_loop(
                0, n_prompt, lambda c, p: score_step(c, p, tp, 0, 0, None, False), peak
            )
        skip = n_prompt * CHUNK
        peak = lax.fori_loop(
            0, n_own, lambda c, p: score_step(c, p, rows, koff, skip, lim, True), peak
        )
        peak = jnp.max(peak, axis=0, keepdims=True)
        ot[tile] = jnp.zeros((D, lanes), F32)

        def out_step(chunk, sums, rows_k, off, start):
            total, dots = sums
            v = key_chunk(kv, chunk, rows_k, off)
            p = jnp.exp2(s_scr[pl.ds(start + chunk * CHUNK, CHUNK), :] - peak)
            dp = mm(v, grad, NT)
            total = total + jnp.sum(p.reshape(CHUNK // 8, 8, lanes), axis=0)
            dots = dots + jnp.sum((p * dp).reshape(CHUNK // 8, 8, lanes), axis=0)
            ot[tile] += mm(v, p.astype(BF16), TN)
            return total, dots

        sums = (jnp.zeros((8, lanes), F32), jnp.zeros((8, lanes), F32))
        if n_prompt:
            sums = lax.fori_loop(
                0, n_prompt, lambda c, s: out_step(c, s, tp, tp, 0), sums
            )
        sums = lax.fori_loop(0, n_own, lambda c, s: out_step(c, s, rows, voff, skip), sums)
        total = jnp.sum(sums[0], axis=0, keepdims=True)
        dots = jnp.sum(sums[1], axis=0, keepdims=True)
        lane0 = stats_lane(kind, sizes)
        for j in range(first, last):
            a = (j - first) * per
            for k, v in enumerate((peak, total, dots)):
                stats[j, k : k + 1, lane0 : lane0 + per] = v[:, a : a + per]
            stats[j, 3:4, lane0 : lane0 + per] = jnp.broadcast_to(rest, (1, per))


def combine_kernel(sizes, ways, copies, *refs):
    got = refs[:ways]
    out, margin = refs[ways:]
    tp, tr, _ = sizes
    acc = jnp.zeros((1, 1), F32)
    for i in range(ways):
        parts = [got[j][(i - j) % ways] for j in range(ways)]
        peak = functools.reduce(jnp.maximum, [p[0:1] for p in parts])
        scales = [jnp.exp2(p[0:1] - peak) for p in parts]
        total = sum(s * p[1:2] for s, p in zip(scales, parts))
        dots = sum(s * p[2:3] for s, p in zip(scales, parts))
        delta = dots / total
        out[0, i : i + 1] = peak + jnp.log2(total)
        out[1, i : i + 1] = delta
        out[2, i : i + 1] = scales[0] / total
        acc = acc + jnp.sum(delta[:, HEADS * tp :], axis=1, keepdims=True)
    rest = sum(got[j][0, 3:4, 0:1] for j in range(ways)) / copies
    margin[...] = jnp.broadcast_to(BETA * (acc + rest), margin.shape)


def backward_kernel(sizes, ways, where, kv, qs, gs, ot, info, *refs):
    odq, (dkv, acc, dqt) = refs[:ways], refs[ways:]
    tp, tr, groups = sizes
    g, y = where[0], where[1]
    acc[...] = jnp.zeros(acc.shape, F32)

    for tile, (kind, first, last) in enumerate(tile_lanes(sizes, ways)):
        rows = tp if kind < 0 else tr
        qrow = 0 if kind < 0 else tp + kind * tr
        grow = qrow + tp + 2 * tr
        per = HEADS * rows
        lanes = (last - first) * per
        base = row_base(kind, sizes, ways) + first * per
        q = qs[base : base + lanes]
        grad = gs[base : base + lanes]
        lim = limits(kind, first, last, rows, g, y)
        koff, voff = offsets(kind, sizes)
        lane0 = stats_lane(kind, sizes)
        lse, delta, alpha = (
            jnp.concatenate(
                [info[k, j : j + 1, lane0 : lane0 + per] for j in range(first, last)], axis=1
            )
            for k in range(3)
        )
        n_prompt = groups * tp // CHUNK if kind >= 0 else 0
        n_own = g // (CHUNK // rows) + 1
        dqt[...] = jnp.zeros((D, lanes), F32)

        def step(chunk, rows_k, ko, vo, masked):
            n = CHUNK // rows_k
            k = key_chunk(kv, chunk, rows_k, ko)
            v = key_chunk(kv, chunk, rows_k, vo)
            s = mm(k, q, NT) * SCALE2 - lse
            if masked:
                s = hide(s, chunk * CHUNK, lim)
            p = jnp.exp2(s)
            ds = (p * (mm(v, grad, NT) - delta)).astype(BF16)
            blocks = pl.ds(chunk * n, n)
            acc[blocks, vo : vo + rows_k, :] += mm(p.astype(BF16), grad, NN).reshape(n, rows_k, D)
            acc[blocks, ko : ko + rows_k, :] += mm(ds, q, NN).reshape(n, rows_k, D)
            dqt[...] += mm(k, ds, TN)

        if n_prompt:
            pl.loop(0, n_prompt)(lambda c: step(c, tp, 0, tp, False))
        pl.loop(0, n_own)(lambda c: step(c, rows, koff, voff, True))

        for half, whole in ((0, ot[tile] * alpha), (tp + 2 * tr, dqt[...])):
            turned = whole.T.astype(BF16)
            for j in range(first, last):
                for h in range(HEADS):
                    at = (j - first) * per + h * rows
                    odq[j][qrow + half : qrow + half + rows, h * D : (h + 1) * D] = turned[
                        at : at + rows
                    ]
    dkv[:, 0 : 2 * tp + 4 * tr, :] = acc[...].astype(BF16)
    dkv[:, 2 * tp + 4 * tr :, :] = jnp.zeros((groups, 16, D), BF16)


def final_kernel(sizes, ways, terms, mine, *refs):
    others = refs[: ways - 1]
    p_out, r_out, p_dq, r_dq, p_dkv, r_dkv, loss = refs[ways - 1 :]
    tp, tr, groups = sizes
    n = 2 * tp + 4 * tr
    parts = jnp.sum(terms[:, n : n + 16, :].astype(F32), axis=0)
    margin = jnp.sum(parts[0:8], axis=0, keepdims=True)
    z = -margin
    loss[...] = jnp.maximum(z, 0.0) + jnp.log1p(jnp.exp(-jnp.abs(z)))
    weight = -BETA / (1.0 + jnp.exp(margin))
    weight = weight[:, 0:1]

    def gathered(a, b):
        return mine[a:b].astype(F32) + sum(o[a:b].astype(F32) for o in others)

    half = tp + 2 * tr
    p_out[...] = gathered(0, tp).astype(BF16)
    p_dq[...] = (gathered(half, half + tp) * (weight * SCALE)).astype(BF16)
    for s in range(2):
        a = tp + s * tr
        r_out[s] = gathered(a, a + tr).astype(BF16)
        r_dq[s] = (gathered(half + a, half + a + tr) * (weight * SCALE)).astype(BF16)

    def summed(a, b, scale):
        return (jnp.sum(terms[:, a:b, :].astype(F32), axis=0) * scale).astype(BF16)

    for i, scale in enumerate((weight * SCALE, weight)):
        p_dkv[i] = summed(i * tp, (i + 1) * tp, scale)
        for s in range(2):
            a = 2 * tp + (2 * i + s) * tr
            r_dkv[i, s] = summed(a, a + tr, scale)


VMEM = pl.BlockSpec(memory_space=pltpu.VMEM)
SMEM = pl.BlockSpec(memory_space=pltpu.SMEM)


def call(body, out_shape, ins, scratch=(), limit=56, cost=None):
    return pl.pallas_call(
        body,
        out_shape=out_shape,
        in_specs=ins,
        out_specs=jax.tree.map(lambda _: VMEM, out_shape),
        scratch_shapes=list(scratch),
        cost_estimate=cost,
        compiler_params=pltpu.CompilerParams(vmem_limit_bytes=limit * 1024 * 1024),
    )


def shift(x, axis, by):
    n = lax.axis_size(axis)
    return lax.ppermute(x, axis, [(i, (i + by) % n) for i in range(n)])


def per_device(pq, pkv, rq, rkv, labels, logp, probe, pprobe):
    tp, tr = pq.shape[0], rq.shape[1]
    groups, ways = lax.axis_size("prompt"), lax.axis_size("resp")
    copies = lax.axis_size("dp")
    sizes = (tp, tr, groups)
    wide = HEADS * D
    n = 2 * tp + 4 * tr
    half = tp + 2 * tr
    lanes = HEADS * half
    sds = jax.ShapeDtypeStruct
    where = jnp.stack([lax.axis_index("prompt"), lax.axis_index("resp")]).astype(jnp.int32)

    qg, kvb = call(
        functools.partial(pack_kernel, sizes),
        (sds((2 * half, wide), BF16), sds((groups, n, D), BF16)),
        [VMEM] * 7,
    )(pq, pkv, rq, rkv, labels, probe, pprobe)
    qgs = [qg] + [shift(qg, "resp", j) for j in range(1, ways)]
    kv = lax.all_to_all(kvb, "prompt", 0, 0, tiled=True)

    tiles = len(tile_lanes(sizes, ways))
    tile = ways * lanes // tiles
    qs, gs, ot, stats = call(
        functools.partial(forward_kernel, sizes, ways),
        (
            sds((ways * lanes, D), BF16),
            sds((ways * lanes, D), BF16),
            sds((tiles, D, tile), F32),
            sds((ways, 4, lanes), F32),
        ),
        [SMEM] + [VMEM] * (3 + ways),
        [pltpu.VMEM((groups * (tp + tr), tile), F32)],
        cost=pl.CostEstimate(flops=4_000_000_000, bytes_accessed=8_000_000, transcendentals=0),
    )(where, labels, logp, kv, *qgs)
    all_stats = [stats] + [shift(stats, "resp", j) for j in range(1, ways)]
    info, margin = call(
        functools.partial(combine_kernel, sizes, ways, copies),
        (sds((3, ways, lanes), F32), sds((8, D), F32)),
        [VMEM] * ways,
    )(*all_stats)
    margins = [margin] + [shift(margin, "dp", j) for j in range(1, copies)]

    *odq, dkv = call(
        functools.partial(backward_kernel, sizes, ways),
        (*[sds((2 * half, wide), BF16)] * ways, sds((groups, n + 16, D), BF16)),
        [SMEM] + [VMEM] * 5,
        [pltpu.VMEM((groups, n, D), F32), pltpu.VMEM((D, tile), F32)],
        cost=pl.CostEstimate(flops=7_000_000_000, bytes_accessed=10_000_000, transcendentals=0),
    )(where, kv, qs, gs, ot, info)

    whole = sum(margins)[0:1]
    hi = whole.astype(BF16)
    left = whole - hi.astype(F32)
    mid = left.astype(BF16)
    low = (left - mid.astype(F32)).astype(BF16)
    row = jnp.concatenate([hi, mid, low, jnp.zeros((13, D), BF16)], axis=0)
    dkv = lax.dynamic_update_slice(
        dkv, jnp.broadcast_to(row[None], (groups, 16, D)), (0, n, 0)
    )
    others = [shift(odq[j], "resp", -j) for j in range(1, ways)]
    terms = lax.all_to_all(dkv, "prompt", 0, 0, tiled=True)

    outs = call(
        functools.partial(final_kernel, sizes, ways),
        (
            sds(pq.shape, BF16),
            sds(rq.shape, BF16),
            sds(pq.shape, BF16),
            sds(rq.shape, BF16),
            sds(pkv.shape, BF16),
            sds(rkv.shape, BF16),
            sds((1, D), F32),
        ),
        [VMEM] * (1 + ways),
    )(terms, odq[0], *others)
    return (*outs[:6], outs[6][0, 0])


def solution(mesh):
    placed = (
        P(("prompt", "resp"), "dp"),
        P(None, ("prompt", "resp"), "dp"),
        P(None, ("prompt", "resp"), "dp"),
        P(None, None, ("prompt", "resp"), "dp"),
        P(None, ("prompt", "resp")),
        P(None, ("prompt", "resp")),
        P(None, ("prompt", "resp"), "dp"),
        P(("prompt", "resp"), "dp"),
    )
    return jax.shard_map(
        per_device,
        mesh=mesh,
        in_specs=placed,
        out_specs=(
            P(("prompt", "resp"), "dp"),
            P(None, ("prompt", "resp"), "dp"),
            P(("prompt", "resp"), "dp"),
            P(None, ("prompt", "resp"), "dp"),
            P(None, ("prompt", "resp"), "dp"),
            P(None, None, ("prompt", "resp"), "dp"),
            P(),
        ),
        check_vma=False,
    )
```

time: 1620 us -> 137 us (0.08)
  waiting for transfers between devices: 1300 us -> 48.6 us
  matrix products: 120 us -> 0 us
  blocking collectives: 92.2 us -> 0 us
  other arithmetic: 68 us -> 0.67 us
  starting transfers between devices: 0.16 us -> 48.2 us
  Pallas kernels: 0 us -> 35.5 us
    reduce_scatter x2 -> x0, waiting for transfers between devices: 701 us -> none  [the longest x1 381 us: per_device(): lax.psum_scatter(flat_prompt, ('prompt', 'resp'), scatter_dimension=1, ti...]
    all_gather x2 -> x0, waiting for transfers between devices: 599 us -> none  [the longest x1 302 us: per_device(): lax.all_gather(prompt_key_value, ('prompt', 'resp'), axis=1, tiled=True)]
    dot_general x133 -> x0, matrix products: 120 us -> none  [the longest x38 43.5 us: visible_scores(): jnp.einsum('qkgd,nkd->kgqn', queries, kblock, preferred_element_type=jnp....]
    psum x1 -> x0, blocking collectives: 92.2 us -> none  [per_device(): margin = BETA * lax.psum(partial_margin, ('dp', 'prompt', 'resp'))]
    ppermute x0 -> x12, waiting for transfers between devices: none -> 44 us  [shift(): return lax.ppermute(x, axis, [(i, (i + by) % n) for i in range(n)])]
    dynamic_update_slice x19 -> x0, other arithmetic: 36.8 us -> none  [grad_step(): lax.dynamic_update_slice_in_dim(grad_terms, old_terms + jnp.stack([dkey_b...]
    pallas_call x0 -> x5, Pallas kernels: none -> 35.5 us  [the longest x1 15.1 us: per_device(): call(functools.partial(backward_kernel, sizes, ways), (*[sds((2 * half, w...]
    all_to_all x0 -> x2, starting transfers between devices: none -> 27.2 us  [the longest x1 17.9 us: per_device(): terms = lax.all_to_all(dkv, 'prompt', 0, 0, tiled=True)]
  transfers between devices with their start and end apart: 4 -> 14, of which waited for: 4 -> 9; matrix products, arithmetic and copies ran while one was open for 1% -> 0% of each run, Pallas kernels for 0% -> 11%
where the time goes in v1:
time: 137 us
  waiting for transfers between devices  48.6 us (35%)
  starting transfers between devices  48.2 us (35%)
  Pallas kernels  35.5 us (26%)
  local copies, waits for them, and re-layouts  3.38 us (2%)
    ppermute x12, waiting for transfers between devices, shift(): return lax.ppermute(x, axis, [(i, (i + by) % n) for i in range(n)])  44 us
    ppermute x12, starting transfers between devices, shift(): return lax.ppermute(x, axis, [(i, (i + by) % n) for i in range(n)])  21 us
    all_to_all x1, starting transfers between devices, per_device(): terms = lax.all_to_all(dkv, 'prompt', 0, 0, tiled=True)  17.9 us
    pallas_call x1, Pallas kernels, per_device(): call(functools.partial(backward_kernel, sizes, ways), (*[sds((2 * half, w...  15.1 us
    pallas_call x1, Pallas kernels, per_device(): call(functools.partial(forward_kernel, sizes, ways), (sds((ways * lanes,...  13.3 us
    all_to_all x1, starting transfers between devices, per_device(): kv = lax.all_to_all(kvb, 'prompt', 0, 0, tiled=True)  9.34 us
    all_to_all x1, waiting for transfers between devices, per_device(): terms = lax.all_to_all(dkv, 'prompt', 0, 0, tiled=True)  3.11 us
    pallas_call x1, Pallas kernels, per_device(): call(functools.partial(final_kernel, sizes, ways), (sds(pq.shape, BF16),...  2.97 us
  transfers between devices with their start and end apart: 14, of which 9 were waited for; matrix products, arithmetic and copies ran while one was open for 0% of the time, Pallas kernels for 11%

profile of v1, /device:TPU:4, one launch (start us, length us, event | category | flops | bytes accessed | tf_op | source)
XLA Modules:
  0.0 137.1 jit_solution(10073803769584138424)
XLA Ops:
  0.6 2.5 %shard_map.135 = (bf16[256,1024]{1,0:T(8,128)(2,1)}, bf16[16,256,128]{2,1,0:T(8,128)(2,1)}) custom-call(bf16[64,1024]{1,0:T(8,128)(2,1)} %pq.1, bf16[2,64,128]{2,1,0:T(8,128)(2,1)} %pkv.1, bf16[2,32,1024]{2,1,0:T(8,128)(2,1)} %rq.1, bf16[2,2,32,128]{3,2,1,0:T(8,128)(2,1)} %rkv.1, s32[2,32]{1,0:T(2,128)} %labels.3, bf16[2,32,1024]{2,1,0:T(8,128)(2,1)} %probe.1, ...), custom_call_target="tpu_custom_call" | custom-call | tf_op jit(solution)/shard_map/pallas_call | solution.py:323
  3.1 9.3 %all-to-all-start = ((bf16[16,256,128]{2,1,0:T(8,128)(2,1)}), bf16[16,256,128]{2,1,0:T(8,128)(2,1)S(1)}, u32[]{:S(2)}, u32[]{:S(2)}) async-start(bf16[16,256,128]{2,1,0:T(8,128)(2,1)} %get-tuple-element.27), calls=%async_computation | async-start | bytes 2097152 | tf_op jit(solution)/shard_map/all_to_all | solution.py:329
  12.5 1.7 %collective-permute-start = (bf16[256,1024]{1,0:T(8,128)(2,1)S(1)}, bf16[256,1024]{1,0:T(8,128)(2,1)S(1)}, u32[]{:S(2)}, u32[]{:S(2)}) collective-permute-start(bf16[256,1024]{1,0:T(8,128)(2,1)S(1)} %copy-done.10), channel_id=1, source_target_pairs={{0,1},{1,2},{2,3},{3,0},{4,5},{5,6},{6,7},{7,4},{8,9},{9,10},{10,1... | collective-permute-start | bytes 1572872 | tf_op jit(solution)/shard_map/ppermute | solution.py:308
  14.1 2.9 %collective-permute-start.1 = (bf16[256,1024]{1,0:T(8,128)(2,1)S(1)}, bf16[256,1024]{1,0:T(8,128)(2,1)S(1)}, u32[]{:S(2)}, u32[]{:S(2)}) collective-permute-start(bf16[256,1024]{1,0:T(8,128)(2,1)S(1)} %copy-done.10), channel_id=1, source_target_pairs={{0,2},{1,3},{2,0},{3,1},{4,6},{5,7},{6,4},{7,5},{8,10},{9,11},{10,... | collective-permute-start | bytes 1572872 | tf_op jit(solution)/shard_map/ppermute | solution.py:308
  17.0 1.3 collective-permute-start.2
  18.9 8.5 %collective-permute-done.refs_1_ = bf16[256,1024]{1,0:T(8,128)(2,1)S(1)} collective-permute-done((bf16[256,1024]{1,0:T(8,128)(2,1)S(1)}, bf16[256,1024]{1,0:T(8,128)(2,1)S(1)}, u32[]{:S(2)}, u32[]{:S(2)}) %collective-permute-start) | collective-permute-done | bytes 524320 | tf_op jit(solution)/shard_map/ppermute | solution.py:308
  27.5 12.1 %collective-permute-done.1.refs_2_ = bf16[256,1024]{1,0:T(8,128)(2,1)S(1)} collective-permute-done((bf16[256,1024]{1,0:T(8,128)(2,1)S(1)}, bf16[256,1024]{1,0:T(8,128)(2,1)S(1)}, u32[]{:S(2)}, u32[]{:S(2)}) %collective-permute-start.1) | collective-permute-done | bytes 524320 | tf_op jit(solution)/shard_map/ppermute | solution.py:308
  39.6 1.5 %all-to-all-done.kv = bf16[16,256,128]{2,1,0:T(8,128)(2,1)S(1)} async-done(((bf16[16,256,128]{2,1,0:T(8,128)(2,1)}), bf16[16,256,128]{2,1,0:T(8,128)(2,1)S(1)}, u32[]{:S(2)}, u32[]{:S(2)}) %all-to-all-start) | async-done | bytes 1048608 | tf_op jit(solution)/shard_map/all_to_all | solution.py:329
  42.1 13.3 %shard_map.136 = (bf16[4096,128]{1,0:T(8,128)(2,1)}, bf16[4096,128]{1,0:T(8,128)(2,1)}, f32[4,128,1024]{2,1,0:T(8,128)}, f32[4,4,1024]{2,1,0:T(4,128)}) custom-call(s32[2]{0:T(128)} %pad_add_fusion.where, s32[2,32]{1,0:T(2,128)} %labels.3, f32[2,32]{1,0:T(2,128)} %logp.1, bf16[16,256,128]{2,1,0:T(8,128)(2,1)} %copy-done.1, ...), custom_call_target="tpu_custom_call" | custom-call | flops 4000000000 | bytes 8000000 | tf_op jit(solution)/shard_map/pallas_call | solution.py:333
  55.4 1.6 %collective-permute-start.3 = (f32[4,4,1024]{2,1,0:T(4,128)}, f32[4,4,1024]{2,1,0:T(4,128)S(1)}, u32[]{:S(2)}, u32[]{:S(2)}) collective-permute-start(f32[4,4,1024]{2,1,0:T(4,128)} %get-tuple-element.32.refs_0_), channel_id=1, source_target_pairs={{0,1},{1,2},{2,3},{3,0},{4,5},{5,6},{6,7},{7,4},{8,9},{9,10},{10,1... | collective-permute-start | bytes 196616 | tf_op jit(solution)/shard_map/ppermute | solution.py:308
  57.0 2.9 %collective-permute-start.4 = (f32[4,4,1024]{2,1,0:T(4,128)}, f32[4,4,1024]{2,1,0:T(4,128)S(1)}, u32[]{:S(2)}, u32[]{:S(2)}) collective-permute-start(f32[4,4,1024]{2,1,0:T(4,128)} %get-tuple-element.32.refs_0_), channel_id=1, source_target_pairs={{0,2},{1,3},{2,0},{3,1},{4,6},{5,7},{6,4},{7,5},{8,10},{9,11},{10,... | collective-permute-start | bytes 196616 | tf_op jit(solution)/shard_map/ppermute | solution.py:308
  59.9 1.3 collective-permute-start.5
  61.3 1.7 %collective-permute-done.4.refs_2_ = f32[4,4,1024]{2,1,0:T(4,128)S(1)} collective-permute-done((f32[4,4,1024]{2,1,0:T(4,128)}, f32[4,4,1024]{2,1,0:T(4,128)S(1)}, u32[]{:S(2)}, u32[]{:S(2)}) %collective-permute-start.4) | collective-permute-done | bytes 65568 | tf_op jit(solution)/shard_map/ppermute | solution.py:308
  65.0 1.7 %shard_map.137 = (f32[3,4,1024]{2,1,0:T(4,128)}, f32[8,128]{1,0:T(8,128)}) custom-call(f32[4,4,1024]{2,1,0:T(4,128)} %get-tuple-element.32.refs_0_, f32[4,4,1024]{2,1,0:T(4,128)} %copy-done.5, f32[4,4,1024]{2,1,0:T(4,128)} %copy-done.6, f32[4,4,1024]{2,1,0:T(4,128)} %copy-done.7), custom_call_target="tpu_custom_call" | custom-call | tf_op jit(solution)/shard_map/pallas_call | solution.py:346
  67.5 2.9 %collective-permute-start.8 = (f32[8,128]{1,0:T(8,128)}, f32[8,128]{1,0:T(8,128)S(1)}, u32[]{:S(2)}, u32[]{:S(2)}) collective-permute-start(f32[8,128]{1,0:T(8,128)} %get-tuple-element.35), channel_id=1, source_target_pairs={{0,192},{64,0},{128,64},{192,128},{1,193},{65,1},{129,65},{193,129... | collective-permute-start | bytes 12296 | tf_op jit(solution)/shard_map/ppermute | solution.py:308
  70.5 15.1 %shard_map.138 = (bf16[256,1024]{1,0:T(8,128)(2,1)}, bf16[256,1024]{1,0:T(8,128)(2,1)}, bf16[256,1024]{1,0:T(8,128)(2,1)}, bf16[256,1024]{1,0:T(8,128)(2,1)}, bf16[16,272,128]{2,1,0:T(8,128)(2,1)}) custom-call(s32[2]{0:T(128)} %pad_add_fusion.where, bf16[16,256,128]{2,1,0:T(8,128)(2,1)} %copy-done.1, bf16[4096,128]{1,0:T(8,128)(2,1)} %get-tuple-element.29.qs, ...), custom_call_target="tpu_custom_call" | custom-call | flops 7000000000 | bytes 10000000 | tf_op jit(solution)/shard_map/pallas_call | solution.py:353
  86.4 17.9 %all-to-all-start.1 = ((bf16[16,272,128]{2,1,0:T(8,128)(2,1)}), bf16[16,272,128]{2,1,0:T(8,128)(2,1)S(1)}, u32[]{:S(2)}, u32[]{:S(2)}) async-start(bf16[16,272,128]{2,1,0:T(8,128)(2,1)} %broadcast_dynamic-update-slice_fusion), calls=%async_computation.1 | async-start | bytes 2228224 | tf_op jit(solution)/shard_map/all_to_all | solution.py:371
  104.3 2.2 %collective-permute-start.10 = (bf16[256,1024]{1,0:T(8,128)(2,1)}, bf16[256,1024]{1,0:T(8,128)(2,1)S(1)}, u32[]{:S(2)}, u32[]{:S(2)}) collective-permute-start(bf16[256,1024]{1,0:T(8,128)(2,1)} %get-tuple-element.38), channel_id=1, source_target_pairs={{0,2},{1,3},{2,0},{3,1},{4,6},{5,7},{6,4},{7,5},{8,10},{9,11},{10,... | collective-permute-start | bytes 1572872 | tf_op jit(solution)/shard_map/ppermute | solution.py:308
  106.5 1.5 %collective-permute-start.11 = (bf16[256,1024]{1,0:T(8,128)(2,1)}, bf16[256,1024]{1,0:T(8,128)(2,1)S(1)}, u32[]{:S(2)}, u32[]{:S(2)}) collective-permute-start(bf16[256,1024]{1,0:T(8,128)(2,1)} %get-tuple-element.39), channel_id=1, source_target_pairs={{0,1},{1,2},{2,3},{3,0},{4,5},{5,6},{6,7},{7,4},{8,9},{9,10},{10,1... | collective-permute-start | bytes 1572872 | tf_op jit(solution)/shard_map/ppermute | solution.py:308
  108.0 1.7 %collective-permute-start.9 = (bf16[256,1024]{1,0:T(8,128)(2,1)S(1)}, bf16[256,1024]{1,0:T(8,128)(2,1)S(1)}, u32[]{:S(2)}, u32[]{:S(2)}) collective-permute-start(bf16[256,1024]{1,0:T(8,128)(2,1)S(1)} %copy-done.9), channel_id=1, source_target_pairs={{0,3},{1,0},{2,1},{3,2},{4,7},{5,4},{6,5},{7,6},{8,11},{9,8},{10,9... | collective-permute-start | bytes 1572872 | tf_op jit(solution)/shard_map/ppermute | solution.py:308
  109.7 11.3 %collective-permute-done.10.refs_1_ = bf16[256,1024]{1,0:T(8,128)(2,1)S(1)} collective-permute-done((bf16[256,1024]{1,0:T(8,128)(2,1)}, bf16[256,1024]{1,0:T(8,128)(2,1)S(1)}, u32[]{:S(2)}, u32[]{:S(2)}) %collective-permute-start.10) | collective-permute-done | bytes 524320 | tf_op jit(solution)/shard_map/ppermute | solution.py:308
  121.0 8.9 %collective-permute-done.11.refs_2_ = bf16[256,1024]{1,0:T(8,128)(2,1)S(1)} collective-permute-done((bf16[256,1024]{1,0:T(8,128)(2,1)}, bf16[256,1024]{1,0:T(8,128)(2,1)S(1)}, u32[]{:S(2)}, u32[]{:S(2)}) %collective-permute-start.11) | collective-permute-done | bytes 524320 | tf_op jit(solution)/shard_map/ppermute | solution.py:308
  130.0 3.1 %all-to-all-done.1.terms = bf16[16,272,128]{2,1,0:T(8,128)(2,1)S(1)} async-done(((bf16[16,272,128]{2,1,0:T(8,128)(2,1)}), bf16[16,272,128]{2,1,0:T(8,128)(2,1)S(1)}, u32[]{:S(2)}, u32[]{:S(2)}) %all-to-all-start.1) | async-done | bytes 1114144 | tf_op jit(solution)/shard_map/all_to_all | solution.py:371
  134.1 3.0 %shard_map.139 = (bf16[64,1024]{1,0:T(8,128)(2,1)}, bf16[2,32,1024]{2,1,0:T(8,128)(2,1)}, bf16[64,1024]{1,0:T(8,128)(2,1)}, bf16[2,32,1024]{2,1,0:T(8,128)(2,1)}...) custom-call(bf16[16,272,128]{2,1,0:T(8,128)(2,1)} %copy-done, ...), custom_call_target="tpu_custom_call" | custom-call | tf_op jit(solution)/shard_map/pallas_call | solution.py:373
  (45 shorter events, 6.4 us)
Async XLA Ops:
  3.1 9.3 %copy-start.10 = (bf16[256,1024]{1,0:T(8,128)(2,1)S(1)}, bf16[256,1024]{1,0:T(8,128)(2,1)}, u32[]{:S(2)}) copy-start(bf16[256,1024]{1,0:T(8,128)(2,1)} %get-tuple-element.28.refs_0_) | copy-start | bytes 1572868
  3.1 38.0 %all-to-all-start = ((bf16[16,256,128]{2,1,0:T(8,128)(2,1)}), bf16[16,256,128]{2,1,0:T(8,128)(2,1)S(1)}, u32[]{:S(2)}, u32[]{:S(2)}) async-start(bf16[16,256,128]{2,1,0:T(8,128)(2,1)} %get-tuple-element.27), calls=%async_computation | async-start | bytes 2097152 | tf_op jit(solution)/shard_map/all_to_all | solution.py:329
  12.5 15.0 %collective-permute-start = (bf16[256,1024]{1,0:T(8,128)(2,1)S(1)}, bf16[256,1024]{1,0:T(8,128)(2,1)S(1)}, u32[]{:S(2)}, u32[]{:S(2)}) collective-permute-start(bf16[256,1024]{1,0:T(8,128)(2,1)S(1)} %copy-done.10), channel_id=1, source_target_pairs={{0,1},{1,2},{2,3},{3,0},{4,5},{5,6},{6,7},{7,4},{8,9},{9,10},{10,1... | collective-permute-start | bytes 1572872 | tf_op jit(solution)/shard_map/ppermute | solution.py:308
  14.1 25.5 %collective-permute-start.1 = (bf16[256,1024]{1,0:T(8,128)(2,1)S(1)}, bf16[256,1024]{1,0:T(8,128)(2,1)S(1)}, u32[]{:S(2)}, u32[]{:S(2)}) collective-permute-start(bf16[256,1024]{1,0:T(8,128)(2,1)S(1)} %copy-done.10), channel_id=1, source_target_pairs={{0,2},{1,3},{2,0},{3,1},{4,6},{5,7},{6,4},{7,5},{8,10},{9,11},{10,... | collective-permute-start | bytes 1572872 | tf_op jit(solution)/shard_map/ppermute | solution.py:308
  17.0 22.6 %collective-permute-start.2 = (bf16[256,1024]{1,0:T(8,128)(2,1)S(1)}, bf16[256,1024]{1,0:T(8,128)(2,1)S(1)}, u32[]{:S(2)}, u32[]{:S(2)}) collective-permute-start(bf16[256,1024]{1,0:T(8,128)(2,1)S(1)} %copy-done.10), channel_id=1, source_target_pairs={{0,3},{1,0},{2,1},{3,2},{4,7},{5,4},{6,5},{7,6},{8,11},{9,8},{10,9... | collective-permute-start | bytes 1572872 | tf_op jit(solution)/shard_map/ppermute | solution.py:308
  27.5 13.6 %copy-start.11 = (bf16[256,1024]{1,0:T(8,128)(2,1)}, bf16[256,1024]{1,0:T(8,128)(2,1)S(1)}, u32[]{:S(2)}) copy-start(bf16[256,1024]{1,0:T(8,128)(2,1)S(1)} %collective-permute-done.refs_1_) | copy-start | bytes 1572868
  39.6 1.5 %copy-start.12 = (bf16[256,1024]{1,0:T(8,128)(2,1)}, bf16[256,1024]{1,0:T(8,128)(2,1)S(1)}, u32[]{:S(2)}) copy-start(bf16[256,1024]{1,0:T(8,128)(2,1)S(1)} %collective-permute-done.1.refs_2_) | copy-start | bytes 1572868
  39.6 1.5 %copy-start.13 = (bf16[256,1024]{1,0:T(8,128)(2,1)}, bf16[256,1024]{1,0:T(8,128)(2,1)S(1)}, u32[]{:S(2)}) copy-start(bf16[256,1024]{1,0:T(8,128)(2,1)S(1)} %collective-permute-done.2.refs_3_) | copy-start | bytes 1572868
  55.4 5.9 %collective-permute-start.3 = (f32[4,4,1024]{2,1,0:T(4,128)}, f32[4,4,1024]{2,1,0:T(4,128)S(1)}, u32[]{:S(2)}, u32[]{:S(2)}) collective-permute-start(f32[4,4,1024]{2,1,0:T(4,128)} %get-tuple-element.32.refs_0_), channel_id=1, source_target_pairs={{0,1},{1,2},{2,3},{3,0},{4,5},{5,6},{6,7},{7,4},{8,9},{9,10},{10,1... | collective-permute-start | bytes 196616 | tf_op jit(solution)/shard_map/ppermute | solution.py:308
  57.0 6.1 %collective-permute-start.4 = (f32[4,4,1024]{2,1,0:T(4,128)}, f32[4,4,1024]{2,1,0:T(4,128)S(1)}, u32[]{:S(2)}, u32[]{:S(2)}) collective-permute-start(f32[4,4,1024]{2,1,0:T(4,128)} %get-tuple-element.32.refs_0_), channel_id=1, source_target_pairs={{0,2},{1,3},{2,0},{3,1},{4,6},{5,7},{6,4},{7,5},{8,10},{9,11},{10,... | collective-permute-start | bytes 196616 | tf_op jit(solution)/shard_map/ppermute | solution.py:308
  59.9 4.5 %collective-permute-start.5 = (f32[4,4,1024]{2,1,0:T(4,128)}, f32[4,4,1024]{2,1,0:T(4,128)S(1)}, u32[]{:S(2)}, u32[]{:S(2)}) collective-permute-start(f32[4,4,1024]{2,1,0:T(4,128)} %get-tuple-element.32.refs_0_), channel_id=1, source_target_pairs={{0,3},{1,0},{2,1},{3,2},{4,7},{5,4},{6,5},{7,6},{8,11},{9,8},{10,9... | collective-permute-start | bytes 196616 | tf_op jit(solution)/shard_map/ppermute | solution.py:308
  61.3 3.0 %copy-start.5 = (f32[4,4,1024]{2,1,0:T(4,128)}, f32[4,4,1024]{2,1,0:T(4,128)S(1)}, u32[]{:S(2)}) copy-start(f32[4,4,1024]{2,1,0:T(4,128)S(1)} %collective-permute-done.3.refs_1_) | copy-start | bytes 196612
  66.7 18.9 %collective-permute-start.6 = (f32[8,128]{1,0:T(8,128)}, f32[8,128]{1,0:T(8,128)S(1)}, u32[]{:S(2)}, u32[]{:S(2)}) collective-permute-start(f32[8,128]{1,0:T(8,128)} %get-tuple-element.35), channel_id=1, source_target_pairs={{0,64},{64,128},{128,192},{192,0},{1,65},{65,129},{129,193},{193,1... | collective-permute-start | bytes 12296 | tf_op jit(solution)/shard_map/ppermute | solution.py:308
  66.7 18.9 %collective-permute-start.7 = (f32[8,128]{1,0:T(8,128)}, f32[8,128]{1,0:T(8,128)S(1)}, u32[]{:S(2)}, u32[]{:S(2)}) collective-permute-start(f32[8,128]{1,0:T(8,128)} %get-tuple-element.35), channel_id=1, source_target_pairs={{0,128},{64,192},{128,0},{192,64},{1,129},{65,193},{129,1},{193,65... | collective-permute-start | bytes 12296 | tf_op jit(solution)/shard_map/ppermute | solution.py:308
  67.5 18.1 %collective-permute-start.8 = (f32[8,128]{1,0:T(8,128)}, f32[8,128]{1,0:T(8,128)S(1)}, u32[]{:S(2)}, u32[]{:S(2)}) collective-permute-start(f32[8,128]{1,0:T(8,128)} %get-tuple-element.35), channel_id=1, source_target_pairs={{0,192},{64,0},{128,64},{192,128},{1,193},{65,1},{129,65},{193,129... | collective-permute-start | bytes 12296 | tf_op jit(solution)/shard_map/ppermute | solution.py:308
  70.5 15.1 %copy-start.8 = (f32[8,128]{1,0:T(8,128)S(1)}, f32[8,128]{1,0:T(8,128)}, u32[]{:S(2)}) copy-start(f32[8,128]{1,0:T(8,128)} %get-tuple-element.35) | copy-start | bytes 12292
  86.4 21.6 %copy-start.9 = (bf16[256,1024]{1,0:T(8,128)(2,1)S(1)}, bf16[256,1024]{1,0:T(8,128)(2,1)}, u32[]{:S(2)}) copy-start(bf16[256,1024]{1,0:T(8,128)(2,1)} %get-tuple-element.37) | copy-start | bytes 1572868
  86.4 46.7 %all-to-all-start.1 = ((bf16[16,272,128]{2,1,0:T(8,128)(2,1)}), bf16[16,272,128]{2,1,0:T(8,128)(2,1)S(1)}, u32[]{:S(2)}, u32[]{:S(2)}) async-start(bf16[16,272,128]{2,1,0:T(8,128)(2,1)} %broadcast_dynamic-update-slice_fusion), calls=%async_computation.1 | async-start | bytes 2228224 | tf_op jit(solution)/shard_map/all_to_all | solution.py:371
  104.3 16.7 %collective-permute-start.10 = (bf16[256,1024]{1,0:T(8,128)(2,1)}, bf16[256,1024]{1,0:T(8,128)(2,1)S(1)}, u32[]{:S(2)}, u32[]{:S(2)}) collective-permute-start(bf16[256,1024]{1,0:T(8,128)(2,1)} %get-tuple-element.38), channel_id=1, source_target_pairs={{0,2},{1,3},{2,0},{3,1},{4,6},{5,7},{6,4},{7,5},{8,10},{9,11},{10,... | collective-permute-start | bytes 1572872 | tf_op jit(solution)/shard_map/ppermute | solution.py:308
  106.5 23.4 %collective-permute-start.11 = (bf16[256,1024]{1,0:T(8,128)(2,1)}, bf16[256,1024]{1,0:T(8,128)(2,1)S(1)}, u32[]{:S(2)}, u32[]{:S(2)}) collective-permute-start(bf16[256,1024]{1,0:T(8,128)(2,1)} %get-tuple-element.39), channel_id=1, source_target_pairs={{0,1},{1,2},{2,3},{3,0},{4,5},{5,6},{6,7},{7,4},{8,9},{9,10},{10,1... | collective-permute-start | bytes 1572872 | tf_op jit(solution)/shard_map/ppermute | solution.py:308
  108.0 22.0 %collective-permute-start.9 = (bf16[256,1024]{1,0:T(8,128)(2,1)S(1)}, bf16[256,1024]{1,0:T(8,128)(2,1)S(1)}, u32[]{:S(2)}, u32[]{:S(2)}) collective-permute-start(bf16[256,1024]{1,0:T(8,128)(2,1)S(1)} %copy-done.9), channel_id=1, source_target_pairs={{0,3},{1,0},{2,1},{3,2},{4,7},{5,4},{6,5},{7,6},{8,11},{9,8},{10,9... | collective-permute-start | bytes 1572872 | tf_op jit(solution)/shard_map/ppermute | solution.py:308
  121.0 12.2 %copy-start.2 = (bf16[256,1024]{1,0:T(8,128)(2,1)}, bf16[256,1024]{1,0:T(8,128)(2,1)S(1)}, u32[]{:S(2)}) copy-start(bf16[256,1024]{1,0:T(8,128)(2,1)S(1)} %collective-permute-done.10.refs_1_) | copy-start | bytes 1572868
  129.8 3.3 %copy-start.3 = (bf16[256,1024]{1,0:T(8,128)(2,1)}, bf16[256,1024]{1,0:T(8,128)(2,1)S(1)}, u32[]{:S(2)}) copy-start(bf16[256,1024]{1,0:T(8,128)(2,1)S(1)} %collective-permute-done.11.refs_2_) | copy-start | bytes 1572868
  130.0 3.1 %copy-start.4 = (bf16[256,1024]{1,0:T(8,128)(2,1)}, bf16[256,1024]{1,0:T(8,128)(2,1)S(1)}, u32[]{:S(2)}) copy-start(bf16[256,1024]{1,0:T(8,128)(2,1)S(1)} %collective-permute-done.9.refs_0_) | copy-start | bytes 1572868
  (4 other events, 4.0 us)

commit v2 on v1

v2 whole, which is shorter than its diff:
```python
import functools
import math

import jax
import jax.numpy as jnp
from jax import lax
from jax.experimental import pallas as pl
from jax.experimental.pallas import tpu as pltpu
from jax.sharding import PartitionSpec as P

QUERY_HEADS = 32
KEY_VALUE_HEADS = 4
HEAD_SIZE = 128
BETA = 0.1
HIDDEN = -1e30
FLOOR = -1e29
SCALE = HEAD_SIZE ** -0.5
SCALE2 = SCALE * math.log2(math.e)

HEADS = QUERY_HEADS // KEY_VALUE_HEADS
D = HEAD_SIZE
BF16 = jnp.bfloat16
F32 = jnp.float32
CHUNK = 512

NT = (((1,), (1,)), ((), ()))
TN = (((0,), (0,)), ((), ()))
NN = (((1,), (0,)), ((), ()))


def mm(a, b, dims):
    return lax.dot_general(a, b, dims, preferred_element_type=F32)


def counted_rows(labels):
    row = lax.broadcasted_iota(jnp.int32, labels.shape, 0)
    return labels.astype(F32) * jnp.where(row == 0, 1.0, -1.0)


def as_column(row):
    n = row.shape[1]
    r = lax.broadcasted_iota(jnp.int32, (n, n), 0)
    c = lax.broadcasted_iota(jnp.int32, (n, n), 1)
    return jnp.sum(jnp.where(r == c, jnp.broadcast_to(row, (n, n)), 0.0), axis=1, keepdims=True)


def pack_kernel(sizes, pq, pkv, rq, rkv, labels, logp, probe, pprobe, *refs):
    qg, kvb, rest, kv_in, rkv_in, labels_in, logp_in, probe_in, sems = refs
    tp, tr, groups = sizes
    half = tp + 2 * tr
    moves = [
        (pkv, kv_in),
        (rkv, rkv_in),
        (labels, labels_in),
        (probe, probe_in),
        (logp, logp_in),
        (pq, qg.at[0:tp]),
        (rq.at[0], qg.at[tp : tp + tr]),
        (rq.at[1], qg.at[tp + tr : half]),
        (pprobe, qg.at[half : half + tp]),
    ]
    copies = [pltpu.make_async_copy(a, b, sems.at[i]) for i, (a, b) in enumerate(moves)]
    for copy in copies:
        copy.start()
    copies[0].wait()
    copies[1].wait()
    for g in range(groups):
        for i in range(2):
            kvb[g, i * tp : (i + 1) * tp] = kv_in[i]
            for s in range(2):
                base = 2 * tp + (2 * i + s) * tr
                kvb[g, base : base + tr] = rkv_in[i, s]
    copies[2].wait()
    copies[3].wait()
    counted = counted_rows(labels_in[...])
    for s in range(2):
        col = as_column(counted[s : s + 1])
        base = half + tp + s * tr
        qg[base : base + tr] = (probe_in[s].astype(F32) * col).astype(BF16)
    copies[4].wait()
    rest[...] = jnp.broadcast_to(
        jnp.sum(counted * logp_in[...], axis=(0, 1), keepdims=True), rest.shape
    )
    for copy in copies[5:]:
        copy.wait()


def key_rows(kv, rows, base, chunk):
    n = CHUNK // rows
    return kv[chunk * n : (chunk + 1) * n, base : base + rows, :].reshape(CHUNK, D)


def limits(rows, slot):
    g, y = lax.axis_index("prompt"), lax.axis_index("resp")
    if slot == 0:
        lane = lax.broadcasted_iota(jnp.int32, (1, HEADS * rows), 1)
        return g * rows + lane % rows + 1
    return jnp.full((1, HEADS * rows), g * rows + jnp.where(slot > y, rows, 0), jnp.int32)


def hide(s, start, lim):
    key = lax.broadcasted_iota(jnp.int32, s.shape, 0) + start
    return jnp.where(key < lim, s, HIDDEN)


def pieces(sizes):
    tp, tr, _ = sizes
    half = tp + 2 * tr
    out = [(tp, 0, 0, 0, tp)]
    for s in range(2):
        out.append((tr, HEADS * (tp + s * tr), tp + s * tr, 2 * tp + s * tr, 2 * tp + (2 + s) * tr))
    return out


def steps(sizes):
    tp, tr, groups = sizes
    full = HEADS * (tp + 2 * tr)
    out = [(0, c, 0, full, 0, HEADS * tp) for c in range(groups * tp // CHUNK)]
    for kind, (rows, lane, *_) in enumerate(pieces(sizes)):
        if kind:
            wide = HEADS * rows
            out += [(kind, c, lane, lane + wide, lane, lane + wide) for c in range(groups * rows // CHUNK)]
    return out


def scores(kv, q, sizes, step, lim):
    kind, chunk, a, b, ma, mb = step
    rows, _, _, koff, _ = pieces(sizes)[kind]
    s = mm(key_rows(kv, rows, koff, chunk), q[a:b], NT)
    shown = hide(s[:, : mb - ma], chunk * CHUNK, lim[kind])
    return shown if mb == b else jnp.concatenate([shown, s[:, mb - ma :]], axis=1)


def forward_kernel(sizes, slot, kv, qg, *refs):
    if slot == 0:
        rest, qs, gs, ot, stats, s_scr = refs
        stats[...] = jnp.zeros(stats.shape, F32)
    else:
        _, qs, gs, ot, stats, s_scr = refs
    tp, tr, groups = sizes
    half = tp + 2 * tr
    lanes = HEADS * half
    for rows, lane, row, _, _ in pieces(sizes):
        for h in range(HEADS):
            at = lane + h * rows
            qs[at : at + rows] = qg[row : row + rows, h * D : (h + 1) * D]
            gs[at : at + rows] = qg[half + row : half + row + rows, h * D : (h + 1) * D]
    lim = [limits(p[0], slot) for p in pieces(sizes)]
    todo = steps(sizes)

    peak = jnp.full((8, lanes), FLOOR, F32)
    for i, step in enumerate(todo):
        a, b = step[2:4]
        s = scores(kv, qs, sizes, step, lim)
        s_scr[i * CHUNK : (i + 1) * CHUNK, a:b] = s
        top = jnp.max(s.reshape(CHUNK // 8, 8, b - a), axis=0)
        peak = jnp.maximum(peak, top) if b - a == lanes else over(peak, top, a, b, jnp.maximum)
    peak = jnp.max(peak, axis=0, keepdims=True) * SCALE2

    total = jnp.zeros((8, lanes), F32)
    out = jnp.zeros((D, lanes), F32)
    for i, step in enumerate(todo):
        kind, chunk, a, b = step[:4]
        rows, _, _, _, voff = pieces(sizes)[kind]
        p = jnp.exp2(s_scr[i * CHUNK : (i + 1) * CHUNK, a:b] * SCALE2 - peak[:, a:b])
        part = mm(key_rows(kv, rows, voff, chunk), p.astype(BF16), TN)
        out = over(out, part, a, b, jnp.add)
        total = over(total, jnp.sum(p.reshape(CHUNK // 8, 8, b - a), axis=0), a, b, jnp.add)
    total = jnp.sum(total, axis=0, keepdims=True)
    ot[...] = out
    dots = jnp.sum(out * gs[...].astype(F32).T, axis=0, keepdims=True)
    stats[slot, 0:1] = peak
    stats[slot, 1:2] = total
    stats[slot, 2:3] = dots
    if slot == 0:
        stats[slot, 3:4, 0:D] = rest[0:1]


def over(whole, part, a, b, op):
    n = whole.shape[1]
    cut = [whole[:, :a]] if a else []
    cut.append(op(whole[:, a:b], part))
    if b < n:
        cut.append(whole[:, b:])
    return cut[0] if len(cut) == 1 else jnp.concatenate(cut, axis=1)


def combine_kernel(sizes, ways, copies, *refs):
    got = refs[:ways]
    info, margin = refs[ways:]
    tp = sizes[0]
    acc = jnp.zeros((1, 1), F32)
    for i in range(ways):
        parts = [got[j][(i - j) % ways] for j in range(ways)]
        peak = functools.reduce(jnp.maximum, [p[0:1] for p in parts])
        scales = [jnp.exp2(p[0:1] - peak) for p in parts]
        total = sum(s * p[1:2] for s, p in zip(scales, parts))
        delta = sum(s * p[2:3] for s, p in zip(scales, parts)) / total
        info[i, 0:1] = peak + jnp.log2(total)
        info[i, 1:2] = delta
        info[i, 2:3] = scales[0] / total
        acc = acc + jnp.sum(delta[:, HEADS * tp :], axis=1, keepdims=True)
    rest = sum(got[j][0, 3:4, 0:1] for j in range(ways)) / copies
    margin[...] = jnp.broadcast_to(BETA * (acc + rest), margin.shape)


def backward_kernel(sizes, slot, first, last, kv, qs, gs, ot, info, *refs):
    if first:
        odq, acc = refs
    elif last:
        *margins, before, odq, dkv = refs
    else:
        before, odq, acc = refs
    tp, tr, groups = sizes
    half = tp + 2 * tr
    n = 2 * tp + 4 * tr
    lanes = HEADS * half
    lim = [limits(p[0], slot) for p in pieces(sizes)]
    lse, delta, alpha = (info[slot, k : k + 1] for k in range(3))

    def put(blocks, off, rows, value):
        value = value.reshape(CHUNK // rows, rows, D)
        at = (blocks, slice(off, off + rows), slice(None))
        if not first:
            value = before[at] + value
        if last:
            dkv[at] = value.astype(BF16)
        else:
            acc[at] = value

    dq = jnp.zeros((D, lanes), F32)
    for step in steps(sizes):
        kind, chunk, a, b = step[:4]
        rows, _, _, koff, voff = pieces(sizes)[kind]
        blocks = slice(chunk * (CHUNK // rows), (chunk + 1) * (CHUNK // rows))
        p = jnp.exp2(scores(kv, qs, sizes, step, lim) * SCALE2 - lse[:, a:b])
        dp = mm(key_rows(kv, rows, voff, chunk), gs[a:b], NT)
        ds = (p * (dp - delta[:, a:b])).astype(BF16)
        put(blocks, voff, rows, mm(p.astype(BF16), gs[a:b], NN))
        put(blocks, koff, rows, mm(ds, qs[a:b], NN))
        dq = over(dq, mm(key_rows(kv, rows, koff, chunk), ds, TN), a, b, jnp.add)

    for base, whole in ((0, ot[...] * alpha), (half, dq)):
        turned = whole.T.astype(BF16)
        for rows, lane, row, _, _ in pieces(sizes):
            for h in range(HEADS):
                at = lane + h * rows
                odq[base + row : base + row + rows, h * D : (h + 1) * D] = turned[at : at + rows]
    if last:
        left = sum(m[...] for m in margins)
        row = lax.broadcasted_iota(jnp.int32, (16, D), 0)
        packed = jnp.zeros((16, D), F32)
        for i in range(3):
            part = left.astype(BF16).astype(F32)
            left = left - part
            packed = jnp.where(row == i, jnp.broadcast_to(part[0:1], (16, D)), packed)
        dkv[:, n : n + 16, :] = jnp.broadcast_to(packed.astype(BF16)[None], (groups, 16, D))


def outputs_kernel(sizes, mine, *refs):
    *others, p_out, r_out, dq = refs
    tp, tr, _ = sizes
    half = tp + 2 * tr

    def gathered(a, b):
        return mine[a:b].astype(F32) + sum(o[a:b].astype(F32) for o in others)

    p_out[...] = gathered(0, tp).astype(BF16)
    for s in range(2):
        r_out[s] = gathered(tp + s * tr, tp + (s + 1) * tr).astype(BF16)
    dq[...] = gathered(half, 2 * half)


def final_kernel(sizes, terms, dq, *refs):
    outs, (*held, sems) = refs[:5], refs[5:]
    p_dq, r_dq, p_dkv, r_dkv, loss = held
    tp, tr, groups = sizes
    n = 2 * tp + 4 * tr
    parts = jnp.sum(terms[:, n : n + 16, :].astype(F32), axis=0)
    margin = jnp.sum(parts[0:8], axis=0, keepdims=True)
    z = -margin
    loss[...] = jnp.maximum(z, 0.0) + jnp.log1p(jnp.exp(-jnp.abs(z)))
    weight = (-BETA / (1.0 + jnp.exp(margin)))[:, 0:1]
    copies = [pltpu.make_async_copy(a, b, sems.at[i]) for i, (a, b) in enumerate(zip(held, outs))]
    copies[4].start()
    scaled = weight * SCALE
    p_dq[...] = (dq[0:tp] * scaled).astype(BF16)
    copies[0].start()
    for s in range(2):
        a = tp + s * tr
        r_dq[s] = (dq[a : a + tr] * scaled).astype(BF16)
    copies[1].start()

    def summed(a, b, scale):
        return (jnp.sum(terms[:, a:b, :].astype(F32), axis=0) * scale).astype(BF16)

    for i, scale in enumerate((scaled, weight)):
        p_dkv[i] = summed(i * tp, (i + 1) * tp, scale)
        for s in range(2):
            a = 2 * tp + (2 * i + s) * tr
            r_dkv[i, s] = summed(a, a + tr, scale)
    copies[2].start()
    copies[3].start()
    for copy in copies:
        copy.wait()


VMEM = pl.BlockSpec(memory_space=pltpu.VMEM)
HBM = pl.BlockSpec(memory_space=pltpu.HBM)
sds = jax.ShapeDtypeStruct
held = pltpu.VMEM


def call(body, outs, ins, scratch=(), limit=32, aliases=None, flops=0):
    def run(*args):
        args = [
            pltpu.with_memory_space_constraint(x, pltpu.VMEM) if spec is VMEM else x
            for x, spec in zip(args, ins)
        ]
        return pl.pallas_call(
            body,
            out_shape=outs,
            in_specs=ins,
            out_specs=jax.tree.map(lambda _: VMEM, outs),
            scratch_shapes=list(scratch),
            input_output_aliases=aliases or {},
            cost_estimate=pl.CostEstimate(flops=flops, bytes_accessed=0, transcendentals=0),
            compiler_params=pltpu.CompilerParams(vmem_limit_bytes=limit * 1024 * 1024),
        )(*args)

    return run


def shift(x, axis, by):
    n = lax.axis_size(axis)
    return lax.ppermute(x, axis, [(i, (i + by) % n) for i in range(n)])


def per_device(pq, pkv, rq, rkv, labels, logp, probe, pprobe):
    tp, tr = pq.shape[0], rq.shape[1]
    groups, ways = lax.axis_size("prompt"), lax.axis_size("resp")
    copies = lax.axis_size("dp")
    sizes = (tp, tr, groups)
    wide = HEADS * D
    n = 2 * tp + 4 * tr
    half = tp + 2 * tr
    lanes = HEADS * half

    qg, kvb, rest = pl.pallas_call(
        functools.partial(pack_kernel, sizes),
        out_shape=(held((2 * half, wide), BF16), held((groups, n, D), BF16), held((8, D), F32)),
        in_specs=[HBM] * 8,
        out_specs=(VMEM, VMEM, VMEM),
        scratch_shapes=[
            pltpu.VMEM(pkv.shape, BF16),
            pltpu.VMEM(rkv.shape, BF16),
            pltpu.VMEM(labels.shape, jnp.int32),
            pltpu.VMEM(logp.shape, F32),
            pltpu.VMEM(probe.shape, BF16),
            pltpu.SemaphoreType.DMA((9,)),
        ],
        compiler_params=pltpu.CompilerParams(vmem_limit_bytes=16 * 1024 * 1024),
    )(*[
        pltpu.with_memory_space_constraint(x, pltpu.HBM)
        for x in (pq, pkv, rq, rkv, labels, logp, probe, pprobe)
    ])
    kv = lax.all_to_all(kvb, "prompt", 0, 0, tiled=True)
    order = [0, 1, ways - 1] + list(range(2, ways - 1))
    stats, kept = rest, {}
    for slot in order:
        block = shift(qg, "resp", slot) if slot else qg
        qs, gs, ot, stats = call(
            functools.partial(forward_kernel, sizes, slot),
            (
                held((lanes, D), BF16),
                held((lanes, D), BF16),
                held((D, lanes), F32),
                held((ways, 4, lanes), F32),
            ),
            [VMEM] * 3,
            [pltpu.VMEM((CHUNK * len(steps(sizes)), lanes), F32)],
            aliases={2: 3} if slot else None,
            flops=2 * 2 * groups * half * lanes * D,
        )(kv, block, stats)
        kept[slot] = (qs, gs, ot)
    info, margin = call(
        functools.partial(combine_kernel, sizes, ways, copies),
        (held((ways, 3, lanes), F32), held((8, D), F32)),
        [VMEM] * ways,
    )(stats, *[shift(stats, "resp", j) for j in range(1, ways)])
    margins = [margin] + [shift(margin, "dp", j) for j in range(1, copies)]

    order = order[1:] + [0]
    backs, acc = {}, None
    for slot in order:
        first, last = slot == order[0], slot == order[-1]
        extra = margins if last else []
        if not first:
            extra = extra + [acc]
        end = held((groups, n + 16, D), BF16) if last else held((groups, n, D), F32)
        odq, acc = call(
            functools.partial(backward_kernel, sizes, slot, first, last),
            (held((2 * half, wide), BF16), end),
            [VMEM] * (5 + len(extra)),
            aliases={5: 1} if not first and not last else None,
            flops=5 * 2 * groups * half * lanes * D,
        )(kv, *kept[slot], info, *extra)
        backs[slot] = shift(odq, "resp", -slot) if slot else odq
    terms = lax.all_to_all(acc, "prompt", 0, 0, tiled=True)

    p_out, r_out, dq = call(
        functools.partial(outputs_kernel, sizes),
        (sds(pq.shape, BF16), sds(rq.shape, BF16), held((half, wide), F32)),
        [VMEM] * ways,
    )(*[backs[j] for j in range(ways)])
    last_outs = [
        (pq.shape, BF16),
        (rq.shape, BF16),
        (pkv.shape, BF16),
        (rkv.shape, BF16),
        ((1, D), F32),
    ]
    p_dq, r_dq, p_dkv, r_dkv, loss = pl.pallas_call(
        functools.partial(final_kernel, sizes),
        out_shape=tuple(sds(*o) for o in last_outs),
        in_specs=[VMEM] * 2,
        out_specs=(HBM,) * 5,
        scratch_shapes=[pltpu.VMEM(*o) for o in last_outs] + [pltpu.SemaphoreType.DMA((5,))],
        compiler_params=pltpu.CompilerParams(vmem_limit_bytes=16 * 1024 * 1024),
    )(*[pltpu.with_memory_space_constraint(x, pltpu.VMEM) for x in (terms, dq)])
    return (p_out, r_out, p_dq, r_dq, p_dkv, r_dkv, loss[0, 0])


def solution(mesh):
    placed = (
        P(("prompt", "resp"), "dp"),
        P(None, ("prompt", "resp"), "dp"),
        P(None, ("prompt", "resp"), "dp"),
        P(None, None, ("prompt", "resp"), "dp"),
        P(None, ("prompt", "resp")),
        P(None, ("prompt", "resp")),
        P(None, ("prompt", "resp"), "dp"),
        P(("prompt", "resp"), "dp"),
    )
    return jax.shard_map(
        per_device,
        mesh=mesh,
        in_specs=placed,
        out_specs=(
            P(("prompt", "resp"), "dp"),
            P(None, ("prompt", "resp"), "dp"),
            P(("prompt", "resp"), "dp"),
            P(None, ("prompt", "resp"), "dp"),
            P(None, ("prompt", "resp"), "dp"),
            P(None, None, ("prompt", "resp"), "dp"),
            P(),
        ),
        check_vma=False,
    )
```

time: 137 us -> 113 us (0.82)
  starting transfers between devices: 48.2 us -> 32.8 us
  Pallas kernels: 35.5 us -> 28.5 us
  local copies, waits for them, and re-layouts: 3.38 us -> 0 us
  waiting for transfers between devices: 48.6 us -> 50.8 us
    all_to_all x1, waiting for transfers between devices: 1.51 us -> 23.4 us  [per_device(): kv = lax.all_to_all(kvb, 'prompt', 0, 0, tiled=True)]
    ppermute x12, waiting for transfers between devices: 44 us -> 24.4 us  [shift(): return lax.ppermute(x, axis, [(i, (i + by) % n) for i in range(n)])]
    all_to_all x1, starting transfers between devices: 17.9 us -> 3.7 us  [per_device(): terms = lax.all_to_all(acc, 'prompt', 0, 0, tiled=True)]
    pallas_call x5 -> x12, Pallas kernels: 35.5 us -> 28.5 us  [the longest x10 25.4 us: run(): pl.pallas_call(body, out_shape=outs, in_specs=ins, out_specs=jax.tree.map...]
    unnamed x28 -> x0, local copies, waits for them, and re-layouts: 2.65 us -> none
  transfers between devices with their start and end apart: 14 -> 14, of which waited for: 9 -> 6; matrix products, arithmetic and copies ran while one was open for 0% -> 0% of each run, Pallas kernels for 11% -> 16%
where the time goes in v2:
time: 113 us
  waiting for transfers between devices  50.8 us (45%)
  starting transfers between devices  32.8 us (29%)
  Pallas kernels  28.5 us (25%)
    pallas_call x10, Pallas kernels, run(): pl.pallas_call(body, out_shape=outs, in_specs=ins, out_specs=jax.tree.map...  25.4 us
    ppermute x12, waiting for transfers between devices, shift(): return lax.ppermute(x, axis, [(i, (i + by) % n) for i in range(n)])  24.4 us
    all_to_all x1, waiting for transfers between devices, per_device(): kv = lax.all_to_all(kvb, 'prompt', 0, 0, tiled=True)  23.4 us
    ppermute x12, starting transfers between devices, shift(): return lax.ppermute(x, axis, [(i, (i + by) % n) for i in range(n)])  19.9 us
    all_to_all x1, starting transfers between devices, per_device(): kv = lax.all_to_all(kvb, 'prompt', 0, 0, tiled=True)  9.22 us
    all_to_all x1, starting transfers between devices, per_device(): terms = lax.all_to_all(acc, 'prompt', 0, 0, tiled=True)  3.7 us
    all_to_all x1, waiting for transfers between devices, per_device(): terms = lax.all_to_all(acc, 'prompt', 0, 0, tiled=True)  3.07 us
    pallas_call x1, Pallas kernels, per_device(): pl.pallas_call(functools.partial(pack_kernel, sizes), out_shape=(held((2...  2.27 us
  transfers between devices with their start and end apart: 14, of which 6 were waited for; matrix products, arithmetic and copies ran while one was open for 0% of the time, Pallas kernels for 16%

profile of v2, /device:TPU:4, one launch (start us, length us, event | category | flops | bytes accessed | tf_op | source)
XLA Modules:
  0.0 113.1 jit_solution(11328797803544596647)
XLA Ops:
  0.6 2.3 %shard_map.135 = (bf16[256,1024]{1,0:T(8,128)(2,1)S(1)}, bf16[16,256,128]{2,1,0:T(8,128)(2,1)}, f32[8,128]{1,0:T(8,128)S(1)}) custom-call(bf16[64,1024]{1,0:T(8,128)(2,1)} %pq.1, bf16[2,64,128]{2,1,0:T(8,128)(2,1)} %pkv.1, bf16[2,32,1024]{2,1,0:T(8,128)(2,1)} %rq.1, bf16[2,2,32,128]{3,2,1,0:T(8,128)(2,1)} %rkv.1, s32[2,32]{1,0:T(2,128)} %labels.1, ...), custom_call_target="tpu_custom_call" | custom-call | tf_op jit(solution)/shard_map/pallas_call | solution.py:349
  2.9 9.2 %all-to-all-start = ((bf16[16,256,128]{2,1,0:T(8,128)(2,1)}), bf16[16,256,128]{2,1,0:T(8,128)(2,1)S(1)}, u32[]{:S(2)}, u32[]{:S(2)}) async-start(bf16[16,256,128]{2,1,0:T(8,128)(2,1)} %get-tuple-element.44), calls=%async_computation | async-start | bytes 2097152 | tf_op jit(solution)/shard_map/all_to_all | solution.py:367
  12.1 1.7 %collective-permute-start.2 = (bf16[256,1024]{1,0:T(8,128)(2,1)S(1)}, bf16[256,1024]{1,0:T(8,128)(2,1)S(1)}, u32[]{:S(2)}, u32[]{:S(2)}) collective-permute-start(bf16[256,1024]{1,0:T(8,128)(2,1)S(1)} %get-tuple-element.45.qg), channel_id=1, source_target_pairs={{0,1},{1,2},{2,3},{3,0},{4,5},{5,6},{6,7},{7,4},{8,9},{9,10},{10,1... | collective-permute-start | bytes 1572872 | tf_op jit(solution)/shard_map/ppermute | solution.py:336
  13.8 1.7 %collective-permute-start.1 = (bf16[256,1024]{1,0:T(8,128)(2,1)S(1)}, bf16[256,1024]{1,0:T(8,128)(2,1)S(1)}, u32[]{:S(2)}, u32[]{:S(2)}) collective-permute-start(bf16[256,1024]{1,0:T(8,128)(2,1)S(1)} %get-tuple-element.45.qg), channel_id=1, source_target_pairs={{0,3},{1,0},{2,1},{3,2},{4,7},{5,4},{6,5},{7,6},{8,11},{9,8},{10,9... | collective-permute-start | bytes 1572872 | tf_op jit(solution)/shard_map/ppermute | solution.py:336
  15.5 2.0 %collective-permute-start = (bf16[256,1024]{1,0:T(8,128)(2,1)S(1)}, bf16[256,1024]{1,0:T(8,128)(2,1)S(1)}, u32[]{:S(2)}, u32[]{:S(2)}) collective-permute-start(bf16[256,1024]{1,0:T(8,128)(2,1)S(1)} %get-tuple-element.45.qg), channel_id=1, source_target_pairs={{0,2},{1,3},{2,0},{3,1},{4,6},{5,7},{6,4},{7,5},{8,10},{9,11},{10,... | collective-permute-start | bytes 1572872 | tf_op jit(solution)/shard_map/ppermute | solution.py:336
  17.4 23.4 %all-to-all-done.kv = bf16[16,256,128]{2,1,0:T(8,128)(2,1)S(1)} async-done(((bf16[16,256,128]{2,1,0:T(8,128)(2,1)}), bf16[16,256,128]{2,1,0:T(8,128)(2,1)S(1)}, u32[]{:S(2)}, u32[]{:S(2)}) %all-to-all-start) | async-done | bytes 1048608 | tf_op jit(solution)/shard_map/all_to_all | solution.py:367
  40.8 2.3 %shard_map.136 = (bf16[1024,128]{1,0:T(8,128)(2,1)S(1)}, bf16[1024,128]{1,0:T(8,128)(2,1)S(1)}, f32[128,1024]{1,0:T(8,128)S(1)}, f32[4,4,1024]{2,1,0:T(4,128)S(1)}) custom-call(bf16[16,256,128]{2,1,0:T(8,128)(2,1)S(1)} %all-to-all-done.kv, bf16[256,1024]{1,0:T(8,128)(2,1)S(1)} %get-tuple-element.45.qg, f32[8,128]{1,0:T(8,128)S(1)} %get-tuple-element.46.refs_0_), custom_call_target="tpu_custom_call" | custom-call | flops 1073741824 | tf_op jit(solution)/shard_map/pallas_call | solution.py:320
  43.1 2.2 %shard_map.137 = (bf16[1024,128]{1,0:T(8,128)(2,1)S(1)}, bf16[1024,128]{1,0:T(8,128)(2,1)S(1)}, f32[128,1024]{1,0:T(8,128)S(1)}, f32[4,4,1024]{2,1,0:T(4,128)S(1)}) custom-call(bf16[16,256,128]{2,1,0:T(8,128)(2,1)S(1)} %all-to-all-done.kv, bf16[256,1024]{1,0:T(8,128)(2,1)S(1)} %collective-permute-done.2.qg, ...), custom_call_target="tpu_custom_call", output_to_operand_aliasing={{3}: (2, {})} | custom-call | flops 1073741824 | tf_op jit(solution)/shard_map/pallas_call | solution.py:320
  45.3 2.2 %shard_map.138 = (bf16[1024,128]{1,0:T(8,128)(2,1)S(1)}, bf16[1024,128]{1,0:T(8,128)(2,1)S(1)}, f32[128,1024]{1,0:T(8,128)S(1)}, f32[4,4,1024]{2,1,0:T(4,128)S(1)}) custom-call(bf16[16,256,128]{2,1,0:T(8,128)(2,1)S(1)} %all-to-all-done.kv, bf16[256,1024]{1,0:T(8,128)(2,1)S(1)} %collective-permute-done.1.qg, ...), custom_call_target="tpu_custom_call", output_to_operand_aliasing={{3}: (2, {})} | custom-call | flops 1073741824 | tf_op jit(solution)/shard_map/pallas_call | solution.py:320
  47.5 2.2 %shard_map.139 = (bf16[1024,128]{1,0:T(8,128)(2,1)S(1)}, bf16[1024,128]{1,0:T(8,128)(2,1)S(1)}, f32[128,1024]{1,0:T(8,128)S(1)}, f32[4,4,1024]{2,1,0:T(4,128)S(1)}) custom-call(bf16[16,256,128]{2,1,0:T(8,128)(2,1)S(1)} %all-to-all-done.kv, bf16[256,1024]{1,0:T(8,128)(2,1)S(1)} %collective-permute-done.qg, ...), custom_call_target="tpu_custom_call", output_to_operand_aliasing={{3}: (2, {})} | custom-call | flops 1073741824 | tf_op jit(solution)/shard_map/pallas_call | solution.py:320
  49.7 1.7 %collective-permute-start.3 = (f32[4,4,1024]{2,1,0:T(4,128)S(1)}, f32[4,4,1024]{2,1,0:T(4,128)S(1)}, u32[]{:S(2)}, u32[]{:S(2)}) collective-permute-start(f32[4,4,1024]{2,1,0:T(4,128)S(1)} %get-tuple-element.53.refs_0_), channel_id=1, source_target_pairs={{0,1},{1,2},{2,3},{3,0},{4,5},{5,6},{6,7},{7,4},{8,9},{9,10},{10,1... | collective-permute-start | bytes 196616 | tf_op jit(solution)/shard_map/ppermute | solution.py:336
  51.4 2.9 %collective-permute-start.4 = (f32[4,4,1024]{2,1,0:T(4,128)S(1)}, f32[4,4,1024]{2,1,0:T(4,128)S(1)}, u32[]{:S(2)}, u32[]{:S(2)}) collective-permute-start(f32[4,4,1024]{2,1,0:T(4,128)S(1)} %get-tuple-element.53.refs_0_), channel_id=1, source_target_pairs={{0,2},{1,3},{2,0},{3,1},{4,6},{5,7},{6,4},{7,5},{8,10},{9,11},{10,... | collective-permute-start | bytes 196616 | tf_op jit(solution)/shard_map/ppermute | solution.py:336
  55.6 1.6 %collective-permute-done.4.refs_2_ = f32[4,4,1024]{2,1,0:T(4,128)S(1)} collective-permute-done((f32[4,4,1024]{2,1,0:T(4,128)S(1)}, f32[4,4,1024]{2,1,0:T(4,128)S(1)}, u32[]{:S(2)}, u32[]{:S(2)}) %collective-permute-start.4) | collective-permute-done | bytes 65568 | tf_op jit(solution)/shard_map/ppermute | solution.py:336
  59.7 2.9 %collective-permute-start.8 = (f32[8,128]{1,0:T(8,128)S(1)}, f32[8,128]{1,0:T(8,128)S(1)}, u32[]{:S(2)}, u32[]{:S(2)}) collective-permute-start(f32[8,128]{1,0:T(8,128)S(1)} %get-tuple-element.55.refs_0_), channel_id=1, source_target_pairs={{0,192},{64,0},{128,64},{192,128},{1,193},{65,1},{129,65},{193,129... | collective-permute-start | bytes 12296 | tf_op jit(solution)/shard_map/ppermute | solution.py:336
  62.6 3.4 %shard_map.141 = (bf16[256,1024]{1,0:T(8,128)(2,1)S(1)}, f32[16,256,128]{2,1,0:T(8,128)S(1)}) custom-call(bf16[16,256,128]{2,1,0:T(8,128)(2,1)S(1)} %all-to-all-done.kv, bf16[1024,128]{1,0:T(8,128)(2,1)S(1)} %get-tuple-element.62.qs, bf16[1024,128]{1,0:T(8,128)(2,1)S(1)} %get-tuple-element.63.gs, f32[128,1024]{1,0:T(8,128)S(1)} %get-tuple-element.64.ot, ...), custom_call_target="tpu_custom_call" | custom-call | flops 2684354560 | tf_op jit(solution)/shard_map/pallas_call | solution.py:320
  66.0 3.7 %shard_map.142 = (bf16[256,1024]{1,0:T(8,128)(2,1)S(1)}, f32[16,256,128]{2,1,0:T(8,128)S(1)}) custom-call(bf16[16,256,128]{2,1,0:T(8,128)(2,1)S(1)} %all-to-all-done.kv, bf16[1024,128]{1,0:T(8,128)(2,1)S(1)} %get-tuple-element.59.qs, bf16[1024,128]{1,0:T(8,128)(2,1)S(1)} %get-tuple-element.60.gs, ...), custom_call_target="tpu_custom_call", output_to_operand_aliasing={{1}: (5, {})} | custom-call | flops 2684354560 | tf_op jit(solution)/shard_map/pallas_call | solution.py:320
  69.7 3.6 %shard_map.143 = (bf16[256,1024]{1,0:T(8,128)(2,1)S(1)}, f32[16,256,128]{2,1,0:T(8,128)S(1)}) custom-call(bf16[16,256,128]{2,1,0:T(8,128)(2,1)S(1)} %all-to-all-done.kv, bf16[1024,128]{1,0:T(8,128)(2,1)S(1)} %get-tuple-element.56.qs, bf16[1024,128]{1,0:T(8,128)(2,1)S(1)} %get-tuple-element.57.gs, ...), custom_call_target="tpu_custom_call", output_to_operand_aliasing={{1}: (5, {})} | custom-call | flops 2684354560 | tf_op jit(solution)/shard_map/pallas_call | solution.py:320
  73.4 4.8 %shard_map.144 = (bf16[256,1024]{1,0:T(8,128)(2,1)S(1)}, bf16[16,272,128]{2,1,0:T(8,128)(2,1)}) custom-call(bf16[16,256,128]{2,1,0:T(8,128)(2,1)S(1)} %all-to-all-done.kv, bf16[1024,128]{1,0:T(8,128)(2,1)S(1)} %get-tuple-element.47.qs, bf16[1024,128]{1,0:T(8,128)(2,1)S(1)} %get-tuple-element.48.gs, f32[128,1024]{1,0:T(8,128)S(1)} %get-tuple-element.49.ot, ...), custom_call_target="tpu_custom_call" | custom-call | flops 2684354560 | tf_op jit(solution)/shard_map/pallas_call | solution.py:320
  78.1 3.7 %all-to-all-start.1 = ((bf16[16,272,128]{2,1,0:T(8,128)(2,1)}), bf16[16,272,128]{2,1,0:T(8,128)(2,1)S(1)}, u32[]{:S(2)}, u32[]{:S(2)}) async-start(bf16[16,272,128]{2,1,0:T(8,128)(2,1)} %get-tuple-element.74), calls=%async_computation.1 | async-start | bytes 2228224 | tf_op jit(solution)/shard_map/all_to_all | solution.py:409
  81.8 1.6 %collective-permute-start.10 = (bf16[256,1024]{1,0:T(8,128)(2,1)S(1)}, bf16[256,1024]{1,0:T(8,128)(2,1)S(1)}, u32[]{:S(2)}, u32[]{:S(2)}) collective-permute-start(bf16[256,1024]{1,0:T(8,128)(2,1)S(1)} %get-tuple-element.70), channel_id=1, source_target_pairs={{0,2},{1,3},{2,0},{3,1},{4,6},{5,7},{6,4},{7,5},{8,10},{9,11},{10,... | collective-permute-start | bytes 1572872 | tf_op jit(solution)/shard_map/ppermute | solution.py:336
  83.4 1.9 %collective-permute-start.11 = (bf16[256,1024]{1,0:T(8,128)(2,1)S(1)}, bf16[256,1024]{1,0:T(8,128)(2,1)S(1)}, u32[]{:S(2)}, u32[]{:S(2)}) collective-permute-start(bf16[256,1024]{1,0:T(8,128)(2,1)S(1)} %get-tuple-element.71), channel_id=1, source_target_pairs={{0,1},{1,2},{2,3},{3,0},{4,5},{5,6},{6,7},{7,4},{8,9},{9,10},{10,1... | collective-permute-start | bytes 1572872 | tf_op jit(solution)/shard_map/ppermute | solution.py:336
  86.6 11.7 %collective-permute-done.10.refs_1_ = bf16[256,1024]{1,0:T(8,128)(2,1)S(1)} collective-permute-done((bf16[256,1024]{1,0:T(8,128)(2,1)S(1)}, bf16[256,1024]{1,0:T(8,128)(2,1)S(1)}, u32[]{:S(2)}, u32[]{:S(2)}) %collective-permute-start.10) | collective-permute-done | bytes 524320 | tf_op jit(solution)/shard_map/ppermute | solution.py:336
  98.3 9.8 %collective-permute-done.11.refs_2_ = bf16[256,1024]{1,0:T(8,128)(2,1)S(1)} collective-permute-done((bf16[256,1024]{1,0:T(8,128)(2,1)S(1)}, bf16[256,1024]{1,0:T(8,128)(2,1)S(1)}, u32[]{:S(2)}, u32[]{:S(2)}) %collective-permute-start.11) | collective-permute-done | bytes 524320 | tf_op jit(solution)/shard_map/ppermute | solution.py:336
  108.9 3.1 %all-to-all-done.1.terms = bf16[16,272,128]{2,1,0:T(8,128)(2,1)S(1)} async-done(((bf16[16,272,128]{2,1,0:T(8,128)(2,1)}), bf16[16,272,128]{2,1,0:T(8,128)(2,1)S(1)}, u32[]{:S(2)}, u32[]{:S(2)}) %all-to-all-start.1) | async-done | bytes 1114144 | tf_op jit(solution)/shard_map/all_to_all | solution.py:409
  (16 shorter events, 6.9 us)
Async XLA Ops:
  2.9 37.9 %all-to-all-start = ((bf16[16,256,128]{2,1,0:T(8,128)(2,1)}), bf16[16,256,128]{2,1,0:T(8,128)(2,1)S(1)}, u32[]{:S(2)}, u32[]{:S(2)}) async-start(bf16[16,256,128]{2,1,0:T(8,128)(2,1)} %get-tuple-element.44), calls=%async_computation | async-start | bytes 2097152 | tf_op jit(solution)/shard_map/all_to_all | solution.py:367
  12.1 31.0 %collective-permute-start.2 = (bf16[256,1024]{1,0:T(8,128)(2,1)S(1)}, bf16[256,1024]{1,0:T(8,128)(2,1)S(1)}, u32[]{:S(2)}, u32[]{:S(2)}) collective-permute-start(bf16[256,1024]{1,0:T(8,128)(2,1)S(1)} %get-tuple-element.45.qg), channel_id=1, source_target_pairs={{0,1},{1,2},{2,3},{3,0},{4,5},{5,6},{6,7},{7,4},{8,9},{9,10},{10,1... | collective-permute-start | bytes 1572872 | tf_op jit(solution)/shard_map/ppermute | solution.py:336
  13.8 31.5 %collective-permute-start.1 = (bf16[256,1024]{1,0:T(8,128)(2,1)S(1)}, bf16[256,1024]{1,0:T(8,128)(2,1)S(1)}, u32[]{:S(2)}, u32[]{:S(2)}) collective-permute-start(bf16[256,1024]{1,0:T(8,128)(2,1)S(1)} %get-tuple-element.45.qg), channel_id=1, source_target_pairs={{0,3},{1,0},{2,1},{3,2},{4,7},{5,4},{6,5},{7,6},{8,11},{9,8},{10,9... | collective-permute-start | bytes 1572872 | tf_op jit(solution)/shard_map/ppermute | solution.py:336
  15.5 32.1 %collective-permute-start = (bf16[256,1024]{1,0:T(8,128)(2,1)S(1)}, bf16[256,1024]{1,0:T(8,128)(2,1)S(1)}, u32[]{:S(2)}, u32[]{:S(2)}) collective-permute-start(bf16[256,1024]{1,0:T(8,128)(2,1)S(1)} %get-tuple-element.45.qg), channel_id=1, source_target_pairs={{0,2},{1,3},{2,0},{3,1},{4,6},{5,7},{6,4},{7,5},{8,10},{9,11},{10,... | collective-permute-start | bytes 1572872 | tf_op jit(solution)/shard_map/ppermute | solution.py:336
  49.7 5.9 %collective-permute-start.3 = (f32[4,4,1024]{2,1,0:T(4,128)S(1)}, f32[4,4,1024]{2,1,0:T(4,128)S(1)}, u32[]{:S(2)}, u32[]{:S(2)}) collective-permute-start(f32[4,4,1024]{2,1,0:T(4,128)S(1)} %get-tuple-element.53.refs_0_), channel_id=1, source_target_pairs={{0,1},{1,2},{2,3},{3,0},{4,5},{5,6},{6,7},{7,4},{8,9},{9,10},{10,1... | collective-permute-start | bytes 196616 | tf_op jit(solution)/shard_map/ppermute | solution.py:336
  51.4 5.8 %collective-permute-start.4 = (f32[4,4,1024]{2,1,0:T(4,128)S(1)}, f32[4,4,1024]{2,1,0:T(4,128)S(1)}, u32[]{:S(2)}, u32[]{:S(2)}) collective-permute-start(f32[4,4,1024]{2,1,0:T(4,128)S(1)} %get-tuple-element.53.refs_0_), channel_id=1, source_target_pairs={{0,2},{1,3},{2,0},{3,1},{4,6},{5,7},{6,4},{7,5},{8,10},{9,11},{10,... | collective-permute-start | bytes 196616 | tf_op jit(solution)/shard_map/ppermute | solution.py:336
  54.3 4.3 %collective-permute-start.5 = (f32[4,4,1024]{2,1,0:T(4,128)S(1)}, f32[4,4,1024]{2,1,0:T(4,128)S(1)}, u32[]{:S(2)}, u32[]{:S(2)}) collective-permute-start(f32[4,4,1024]{2,1,0:T(4,128)S(1)} %get-tuple-element.53.refs_0_), channel_id=1, source_target_pairs={{0,3},{1,0},{2,1},{3,2},{4,7},{5,4},{6,5},{7,6},{8,11},{9,8},{10,9... | collective-permute-start | bytes 196616 | tf_op jit(solution)/shard_map/ppermute | solution.py:336
  58.7 14.6 %collective-permute-start.6 = (f32[8,128]{1,0:T(8,128)S(1)}, f32[8,128]{1,0:T(8,128)S(1)}, u32[]{:S(2)}, u32[]{:S(2)}) collective-permute-start(f32[8,128]{1,0:T(8,128)S(1)} %get-tuple-element.55.refs_0_), channel_id=1, source_target_pairs={{0,64},{64,128},{128,192},{192,0},{1,65},{65,129},{129,193},{193,1... | collective-permute-start | bytes 12296 | tf_op jit(solution)/shard_map/ppermute | solution.py:336
  58.8 14.5 %collective-permute-start.7 = (f32[8,128]{1,0:T(8,128)S(1)}, f32[8,128]{1,0:T(8,128)S(1)}, u32[]{:S(2)}, u32[]{:S(2)}) collective-permute-start(f32[8,128]{1,0:T(8,128)S(1)} %get-tuple-element.55.refs_0_), channel_id=1, source_target_pairs={{0,128},{64,192},{128,0},{192,64},{1,129},{65,193},{129,1},{193,65... | collective-permute-start | bytes 12296 | tf_op jit(solution)/shard_map/ppermute | solution.py:336
  59.7 13.6 %collective-permute-start.8 = (f32[8,128]{1,0:T(8,128)S(1)}, f32[8,128]{1,0:T(8,128)S(1)}, u32[]{:S(2)}, u32[]{:S(2)}) collective-permute-start(f32[8,128]{1,0:T(8,128)S(1)} %get-tuple-element.55.refs_0_), channel_id=1, source_target_pairs={{0,192},{64,0},{128,64},{192,128},{1,193},{65,1},{129,65},{193,129... | collective-permute-start | bytes 12296 | tf_op jit(solution)/shard_map/ppermute | solution.py:336
  78.1 33.9 %all-to-all-start.1 = ((bf16[16,272,128]{2,1,0:T(8,128)(2,1)}), bf16[16,272,128]{2,1,0:T(8,128)(2,1)S(1)}, u32[]{:S(2)}, u32[]{:S(2)}) async-start(bf16[16,272,128]{2,1,0:T(8,128)(2,1)} %get-tuple-element.74), calls=%async_computation.1 | async-start | bytes 2228224 | tf_op jit(solution)/shard_map/all_to_all | solution.py:409
  81.8 16.5 %collective-permute-start.10 = (bf16[256,1024]{1,0:T(8,128)(2,1)S(1)}, bf16[256,1024]{1,0:T(8,128)(2,1)S(1)}, u32[]{:S(2)}, u32[]{:S(2)}) collective-permute-start(bf16[256,1024]{1,0:T(8,128)(2,1)S(1)} %get-tuple-element.70), channel_id=1, source_target_pairs={{0,2},{1,3},{2,0},{3,1},{4,6},{5,7},{6,4},{7,5},{8,10},{9,11},{10,... | collective-permute-start | bytes 1572872 | tf_op jit(solution)/shard_map/ppermute | solution.py:336
  83.4 24.7 %collective-permute-start.11 = (bf16[256,1024]{1,0:T(8,128)(2,1)S(1)}, bf16[256,1024]{1,0:T(8,128)(2,1)S(1)}, u32[]{:S(2)}, u32[]{:S(2)}) collective-permute-start(bf16[256,1024]{1,0:T(8,128)(2,1)S(1)} %get-tuple-element.71), channel_id=1, source_target_pairs={{0,1},{1,2},{2,3},{3,0},{4,5},{5,6},{6,7},{7,4},{8,9},{9,10},{10,1... | collective-permute-start | bytes 1572872 | tf_op jit(solution)/shard_map/ppermute | solution.py:336
  85.3 22.8 %collective-permute-start.9 = (bf16[256,1024]{1,0:T(8,128)(2,1)S(1)}, bf16[256,1024]{1,0:T(8,128)(2,1)S(1)}, u32[]{:S(2)}, u32[]{:S(2)}) collective-permute-start(bf16[256,1024]{1,0:T(8,128)(2,1)S(1)} %get-tuple-element.69), channel_id=1, source_target_pairs={{0,3},{1,0},{2,1},{3,2},{4,7},{5,4},{6,5},{7,6},{8,11},{9,8},{10,9... | collective-permute-start | bytes 1572872 | tf_op jit(solution)/shard_map/ppermute | solution.py:336
